TPU v7x, 512 devices: a whole 4x8x8 slice. The times are simulated.
512 devices in a mesh: dp: 64 (over x, z_lo, y), mp: 8 (over z_hi, core).
Axes of the slice: x: 4, y: 8, z: 8 (z_hi: 4, z_lo: 2; z = z_hi * 2 + z_lo), core: 2. Of those that a mesh axis runs over, the one named last changes fastest.
Arguments:
- query_states: bfloat16 [8192, 2048], P('dp'), may hold values from -6 to 6
- passage_states: bfloat16 [8192, 2048], P('dp'), may hold values from -6 to 6
- proj_weight: bfloat16 [2048, 2048], P('dp', 'mp'), may hold values from -0.125 to 0.125
- positive_index: int32 [8192], P('dp'), may hold values from 0 to 127
- logit_scale: float32 [1], replicated, may hold values from 0.01 to 0.04
- logit_bias: float32 [1], replicated, may hold values from -1.5 to 0.5
Outputs:
- grad_queries: float32 [8192, 2048], P('dp', 'mp')
- grad_passages: float32 [8192, 2048], P('dp', 'mp')
All inputs are finite; a program needn't handle non-finite values.
Results may differ from a plain program's by a relative error of at most 0.011.
Values may be sent and summed in bfloat16 or wider, within the bound.
No kernel may reach another device: no remote copies, remote signals or barrier semaphores. Data moves between devices by JAX's collectives and lax.ppermute only.
A program may use at most 64 MiB of HBM per device.

v0:
```python
import jax
import jax.numpy as jnp
from jax import lax
from jax.sharding import PartitionSpec as P


def shifted(block, axis, distance):
    devices = range(lax.axis_size(axis))
    route = [((i - distance) % len(devices), i) for i in devices]
    return lax.ppermute(block, axis, route)


def inner_rows(left, right):
    return lax.dot_general(
        left, right, (((1,), (1,)), ((), ())), preferred_element_type=jnp.float32
    )


def outer_rows(left, right):
    return lax.dot_general(
        left, right, (((0,), (0,)), ((), ())), preferred_element_type=jnp.float32
    )


def per_device(query_states, passage_states, proj_weight, positive_index, logit_scale, logit_bias):
    row_count = query_states.shape[0]
    column_count = proj_weight.shape[1]
    dev_count = lax.axis_size("dp")
    group_size = 8
    turn_count = dev_count // group_size
    zeros_init = jnp.zeros((row_count, column_count), jnp.float32)
    piece = lax.all_gather(proj_weight, "dp", axis=0, tiled=True)
    query_acc = jnp.dot(query_states, piece, preferred_element_type=jnp.float32)
    passage_acc = jnp.dot(passage_states, piece, preferred_element_type=jnp.float32)
    queries = query_acc.astype(jnp.bfloat16)
    passages = passage_acc.astype(jnp.bfloat16)
    scale_value = logit_scale[0]
    bias_value = logit_bias[0]
    column_ids = jnp.arange(row_count, dtype=jnp.int32)
    own_labels = (column_ids[None, :] == positive_index[:, None]).astype(jnp.float32)
    label_rows = jnp.concatenate(
        [own_labels, jnp.zeros((row_count, (group_size - 1) * row_count), jnp.float32)], axis=1
    )

    def tile_weight(scores, labels):
        logits = scale_value * scores + bias_value
        return (jax.nn.sigmoid(logits) - labels).astype(jnp.bfloat16)

    passage_group = passages
    for level in range(3):
        span = 1 << level
        moved_p = shifted(passage_group, "dp", span)
        passage_group = jnp.concatenate([passage_group, moved_p], axis=0)
    group_zeros = jnp.zeros((group_size * row_count, column_count), jnp.float32)

    def one_turn(turn_index, state_in):
        passage_block, grad_acc, grad_q = state_in
        first_turn = (turn_index == 0).astype(jnp.float32)
        next_block = shifted(passage_block, "dp", group_size)
        scores = lax.psum(inner_rows(queries, passage_block).astype(jnp.bfloat16), "mp").astype(
            jnp.float32
        )
        weight = tile_weight(scores, label_rows * first_turn)
        grad_q = grad_q + jnp.dot(weight, passage_block, preferred_element_type=jnp.float32)
        grad_acc = shifted(
            (grad_acc + outer_rows(weight, queries)).astype(jnp.bfloat16), "dp", group_size
        ).astype(jnp.float32)
        return (next_block, grad_acc, grad_q)

    final_state = lax.fori_loop(0, turn_count, one_turn, (passage_group, group_zeros, zeros_init))
    grad_group, grad_q = (final_state[1], final_state[2])
    pending = grad_group.reshape(group_size, row_count, column_count)
    for level in range(3):
        half = pending.shape[0] // 2
        returned = shifted(pending[half:].astype(jnp.bfloat16), "dp", -half).astype(jnp.float32)
        pending = pending[:half] + returned
    grad_p = pending[0]
    return (scale_value * grad_q, scale_value * grad_p)


def solution(mesh):
    in_specs = (P("dp", None), P("dp", None), P("dp", "mp"), P("dp"), P(), P())
    out_specs = (P("dp", "mp"), P("dp", "mp"))
    return jax.shard_map(
        per_device, mesh=mesh, in_specs=in_specs, out_specs=out_specs, check_vma=False
    )
```

profile of v0, /device:TPU:128, one launch (start us, length us, event | category | flops | bytes accessed | tf_op | source)
XLA Modules:
  0.0 1284.5 jit_solution(12425613757195777643)
XLA Ops:
  7.9 305.5 %all-gather.2.cloned.1.call-done = bf16[2048,256]{1,0:T(8,128)(2,1)} async-done(((bf16[32,256]{1,0:T(8,128)(2,1)}), bf16[2048,256]{1,0:T(8,128)(2,1)}) %all-gather.2.cloned.1.call-update) | async-done | bytes 1048592 | tf_op jit(solution)/shard_map/all_gather | solution.py:32
  328.2 10.1 collective-permute-done.3
  341.6 11.9 collective-permute-done.4
  353.6 880.4 %while.18 = (s32[]{:T(128)}, bf16[1024,256]{1,0:T(8,128)(2,1)S(1)}, f32[1024,256]{1,0:T(8,128)S(1)}, f32[128,256]{1,0:T(8,128)}, f32[]{:T(128)}, /*index=5*/bf16...) while((s32[]{:T(128)}, bf16[1024,256]{1,0:T(8,128)(2,1)S(1)}, ...), condition=%wide.region_2.0_spmd.clone, body=%wide.region_0.0_spmd.clone.sunk | while | flops 203882496 | bytes 13238521 | solution.py:70
  354.7 71.2 %all-reduce.3.cloned.1.call-done = bf16[128,1024]{1,0:T(8,128)(2,1)} async-done(((bf16[128,1024]{1,0:T(8,128)(2,1)}), bf16[128,1024]{1,0:T(8,128)(2,1)}) %all-reduce.3.cloned.1.call-update) | async-done | bytes 262160 | tf_op jit(solution)/shard_map/while/body/eval_jaxpr/psum | solution.py:60
  437.1 9.4 collective-permute-done.1
  447.7 10.0 collective-permute-done
  458.7 78.2 %all-reduce.3.cloned.1.call-done = bf16[128,1024]{1,0:T(8,128)(2,1)} async-done(((bf16[128,1024]{1,0:T(8,128)(2,1)}), bf16[128,1024]{1,0:T(8,128)(2,1)}) %all-reduce.3.cloned.1.call-update) | async-done | bytes 262160 | tf_op jit(solution)/shard_map/while/body/eval_jaxpr/psum | solution.py:60
  558.7 10.0 collective-permute-done
  569.8 77.9 %all-reduce.3.cloned.1.call-done = bf16[128,1024]{1,0:T(8,128)(2,1)} async-done(((bf16[128,1024]{1,0:T(8,128)(2,1)}), bf16[128,1024]{1,0:T(8,128)(2,1)}) %all-reduce.3.cloned.1.call-update) | async-done | bytes 262160 | tf_op jit(solution)/shard_map/while/body/eval_jaxpr/psum | solution.py:60
  659.8 8.5 collective-permute-done.1
  669.4 10.0 collective-permute-done
  680.5 77.9 %all-reduce.3.cloned.1.call-done = bf16[128,1024]{1,0:T(8,128)(2,1)} async-done(((bf16[128,1024]{1,0:T(8,128)(2,1)}), bf16[128,1024]{1,0:T(8,128)(2,1)}) %all-reduce.3.cloned.1.call-update) | async-done | bytes 262160 | tf_op jit(solution)/shard_map/while/body/eval_jaxpr/psum | solution.py:60
  770.5 8.5 collective-permute-done.1
  780.1 10.0 collective-permute-done
  791.2 77.9 %all-reduce.3.cloned.1.call-done = bf16[128,1024]{1,0:T(8,128)(2,1)} async-done(((bf16[128,1024]{1,0:T(8,128)(2,1)}), bf16[128,1024]{1,0:T(8,128)(2,1)}) %all-reduce.3.cloned.1.call-update) | async-done | bytes 262160 | tf_op jit(solution)/shard_map/while/body/eval_jaxpr/psum | solution.py:60
  890.8 10.0 collective-permute-done
  901.9 78.2 %all-reduce.3.cloned.1.call-done = bf16[128,1024]{1,0:T(8,128)(2,1)} async-done(((bf16[128,1024]{1,0:T(8,128)(2,1)}), bf16[128,1024]{1,0:T(8,128)(2,1)}) %all-reduce.3.cloned.1.call-update) | async-done | bytes 262160 | tf_op jit(solution)/shard_map/while/body/eval_jaxpr/psum | solution.py:60
  1001.9 10.0 collective-permute-done
  1013.0 78.2 %all-reduce.3.cloned.1.call-done = bf16[128,1024]{1,0:T(8,128)(2,1)} async-done(((bf16[128,1024]{1,0:T(8,128)(2,1)}), bf16[128,1024]{1,0:T(8,128)(2,1)}) %all-reduce.3.cloned.1.call-update) | async-done | bytes 262160 | tf_op jit(solution)/shard_map/while/body/eval_jaxpr/psum | solution.py:60
  1112.9 10.0 collective-permute-done
  1124.0 78.2 %all-reduce.3.cloned.1.call-done = bf16[128,1024]{1,0:T(8,128)(2,1)} async-done(((bf16[128,1024]{1,0:T(8,128)(2,1)}), bf16[128,1024]{1,0:T(8,128)(2,1)}) %all-reduce.3.cloned.1.call-update) | async-done | bytes 262160 | tf_op jit(solution)/shard_map/while/body/eval_jaxpr/psum | solution.py:60
  1223.9 10.0 collective-permute-done
  1250.1 12.4 collective-permute-start.6
  (121 shorter events, 205.4 us)
Async XLA Ops:
  7.2 306.2 %all-gather.2.cloned.1.call-start = ((), (), s32[]{:S(2)}) async-start(), calls=%async_computation | async-start | bytes 1064960 | tf_op jit(solution)/shard_map/all_gather | solution.py:32
  353.6 72.4 %all-reduce.3.cloned.1.call-start = ((), (), s32[]{:S(2)}) async-start(), calls=%async_computation.1 | async-start | bytes 524288 | tf_op jit(solution)/shard_map/while/body/eval_jaxpr/psum | solution.py:60
  429.5 17.1 %collective-permute-start.1 = (bf16[1024,256]{1,0:T(8,128)(2,1)}, bf16[1024,256]{1,0:T(8,128)(2,1)}, u32[]{:S(2)}, u32[]{:S(2)}) collective-permute-start(bf16[1024,256]{1,0:T(8,128)(2,1)} %fusion.26), channel_id=1, source_target_pairs={{448,0},{456,8},{464,16},{472,24},{480,32},{488,40},{496,48},{504,... | collective-permute-start | bytes 1572872 | tf_op jit(solution)/shard_map/while/body/eval_jaxpr/ppermute | solution.py:10
  432.2 25.4 %collective-permute-start = (bf16[1024,256]{1,0:T(8,128)(2,1)S(1)}, bf16[1024,256]{1,0:T(8,128)(2,1)S(1)}, u32[]{:S(2)}, u32[]{:S(2)}) collective-permute-start(bf16[1024,256]{1,0:T(8,128)(2,1)S(1)} %copy.14), channel_id=1, source_target_pairs={{448,0},{456,8},{464,16},{472,24},{480,32},{488,40},{496,48},{504,... | collective-permute-start | bytes 1572872 | tf_op jit(solution)/shard_map/while/body/eval_jaxpr/ppermute | solution.py:10
  457.7 79.3 %all-reduce.3.cloned.1.call-start = ((), (), s32[]{:S(2)}) async-start(), calls=%async_computation.1 | async-start | bytes 524288 | tf_op jit(solution)/shard_map/while/body/eval_jaxpr/psum | solution.py:60
  540.5 17.1 %collective-permute-start.1 = (bf16[1024,256]{1,0:T(8,128)(2,1)}, bf16[1024,256]{1,0:T(8,128)(2,1)}, u32[]{:S(2)}, u32[]{:S(2)}) collective-permute-start(bf16[1024,256]{1,0:T(8,128)(2,1)} %fusion.26), channel_id=1, source_target_pairs={{448,0},{456,8},{464,16},{472,24},{480,32},{488,40},{496,48},{504,... | collective-permute-start | bytes 1572872 | tf_op jit(solution)/shard_map/while/body/eval_jaxpr/ppermute | solution.py:10
  543.3 25.4 %collective-permute-start = (bf16[1024,256]{1,0:T(8,128)(2,1)S(1)}, bf16[1024,256]{1,0:T(8,128)(2,1)S(1)}, u32[]{:S(2)}, u32[]{:S(2)}) collective-permute-start(bf16[1024,256]{1,0:T(8,128)(2,1)S(1)} %copy.14), channel_id=1, source_target_pairs={{448,0},{456,8},{464,16},{472,24},{480,32},{488,40},{496,48},{504,... | collective-permute-start | bytes 1572872 | tf_op jit(solution)/shard_map/while/body/eval_jaxpr/ppermute | solution.py:10
  568.7 79.0 %all-reduce.3.cloned.1.call-start = ((), (), s32[]{:S(2)}) async-start(), calls=%async_computation.1 | async-start | bytes 524288 | tf_op jit(solution)/shard_map/while/body/eval_jaxpr/psum | solution.py:60
  651.2 17.1 %collective-permute-start.1 = (bf16[1024,256]{1,0:T(8,128)(2,1)}, bf16[1024,256]{1,0:T(8,128)(2,1)}, u32[]{:S(2)}, u32[]{:S(2)}) collective-permute-start(bf16[1024,256]{1,0:T(8,128)(2,1)} %fusion.26), channel_id=1, source_target_pairs={{448,0},{456,8},{464,16},{472,24},{480,32},{488,40},{496,48},{504,... | collective-permute-start | bytes 1572872 | tf_op jit(solution)/shard_map/while/body/eval_jaxpr/ppermute | solution.py:10
  654.0 25.4 %collective-permute-start = (bf16[1024,256]{1,0:T(8,128)(2,1)S(1)}, bf16[1024,256]{1,0:T(8,128)(2,1)S(1)}, u32[]{:S(2)}, u32[]{:S(2)}) collective-permute-start(bf16[1024,256]{1,0:T(8,128)(2,1)S(1)} %copy.14), channel_id=1, source_target_pairs={{448,0},{456,8},{464,16},{472,24},{480,32},{488,40},{496,48},{504,... | collective-permute-start | bytes 1572872 | tf_op jit(solution)/shard_map/while/body/eval_jaxpr/ppermute | solution.py:10
  679.4 79.0 %all-reduce.3.cloned.1.call-start = ((), (), s32[]{:S(2)}) async-start(), calls=%async_computation.1 | async-start | bytes 524288 | tf_op jit(solution)/shard_map/while/body/eval_jaxpr/psum | solution.py:60
  762.0 17.1 %collective-permute-start.1 = (bf16[1024,256]{1,0:T(8,128)(2,1)}, bf16[1024,256]{1,0:T(8,128)(2,1)}, u32[]{:S(2)}, u32[]{:S(2)}) collective-permute-start(bf16[1024,256]{1,0:T(8,128)(2,1)} %fusion.26), channel_id=1, source_target_pairs={{448,0},{456,8},{464,16},{472,24},{480,32},{488,40},{496,48},{504,... | collective-permute-start | bytes 1572872 | tf_op jit(solution)/shard_map/while/body/eval_jaxpr/ppermute | solution.py:10
  764.7 25.4 %collective-permute-start = (bf16[1024,256]{1,0:T(8,128)(2,1)S(1)}, bf16[1024,256]{1,0:T(8,128)(2,1)S(1)}, u32[]{:S(2)}, u32[]{:S(2)}) collective-permute-start(bf16[1024,256]{1,0:T(8,128)(2,1)S(1)} %copy.14), channel_id=1, source_target_pairs={{448,0},{456,8},{464,16},{472,24},{480,32},{488,40},{496,48},{504,... | collective-permute-start | bytes 1572872 | tf_op jit(solution)/shard_map/while/body/eval_jaxpr/ppermute | solution.py:10
  790.2 79.0 %all-reduce.3.cloned.1.call-start = ((), (), s32[]{:S(2)}) async-start(), calls=%async_computation.1 | async-start | bytes 524288 | tf_op jit(solution)/shard_map/while/body/eval_jaxpr/psum | solution.py:60
  872.7 17.1 %collective-permute-start.1 = (bf16[1024,256]{1,0:T(8,128)(2,1)}, bf16[1024,256]{1,0:T(8,128)(2,1)}, u32[]{:S(2)}, u32[]{:S(2)}) collective-permute-start(bf16[1024,256]{1,0:T(8,128)(2,1)} %fusion.26), channel_id=1, source_target_pairs={{448,0},{456,8},{464,16},{472,24},{480,32},{488,40},{496,48},{504,... | collective-permute-start | bytes 1572872 | tf_op jit(solution)/shard_map/while/body/eval_jaxpr/ppermute | solution.py:10
  875.4 25.4 %collective-permute-start = (bf16[1024,256]{1,0:T(8,128)(2,1)S(1)}, bf16[1024,256]{1,0:T(8,128)(2,1)S(1)}, u32[]{:S(2)}, u32[]{:S(2)}) collective-permute-start(bf16[1024,256]{1,0:T(8,128)(2,1)S(1)} %copy.14), channel_id=1, source_target_pairs={{448,0},{456,8},{464,16},{472,24},{480,32},{488,40},{496,48},{504,... | collective-permute-start | bytes 1572872 | tf_op jit(solution)/shard_map/while/body/eval_jaxpr/ppermute | solution.py:10
  900.9 79.3 %all-reduce.3.cloned.1.call-start = ((), (), s32[]{:S(2)}) async-start(), calls=%async_computation.1 | async-start | bytes 524288 | tf_op jit(solution)/shard_map/while/body/eval_jaxpr/psum | solution.py:60
  983.7 17.1 %collective-permute-start.1 = (bf16[1024,256]{1,0:T(8,128)(2,1)}, bf16[1024,256]{1,0:T(8,128)(2,1)}, u32[]{:S(2)}, u32[]{:S(2)}) collective-permute-start(bf16[1024,256]{1,0:T(8,128)(2,1)} %fusion.26), channel_id=1, source_target_pairs={{448,0},{456,8},{464,16},{472,24},{480,32},{488,40},{496,48},{504,... | collective-permute-start | bytes 1572872 | tf_op jit(solution)/shard_map/while/body/eval_jaxpr/ppermute | solution.py:10
  986.4 25.4 %collective-permute-start = (bf16[1024,256]{1,0:T(8,128)(2,1)S(1)}, bf16[1024,256]{1,0:T(8,128)(2,1)S(1)}, u32[]{:S(2)}, u32[]{:S(2)}) collective-permute-start(bf16[1024,256]{1,0:T(8,128)(2,1)S(1)} %copy.14), channel_id=1, source_target_pairs={{448,0},{456,8},{464,16},{472,24},{480,32},{488,40},{496,48},{504,... | collective-permute-start | bytes 1572872 | tf_op jit(solution)/shard_map/while/body/eval_jaxpr/ppermute | solution.py:10
  1011.9 79.3 %all-reduce.3.cloned.1.call-start = ((), (), s32[]{:S(2)}) async-start(), calls=%async_computation.1 | async-start | bytes 524288 | tf_op jit(solution)/shard_map/while/body/eval_jaxpr/psum | solution.py:60
  1097.5 25.4 %collective-permute-start = (bf16[1024,256]{1,0:T(8,128)(2,1)S(1)}, bf16[1024,256]{1,0:T(8,128)(2,1)S(1)}, u32[]{:S(2)}, u32[]{:S(2)}) collective-permute-start(bf16[1024,256]{1,0:T(8,128)(2,1)S(1)} %copy.14), channel_id=1, source_target_pairs={{448,0},{456,8},{464,16},{472,24},{480,32},{488,40},{496,48},{504,... | collective-permute-start | bytes 1572872 | tf_op jit(solution)/shard_map/while/body/eval_jaxpr/ppermute | solution.py:10
  1122.9 79.3 %all-reduce.3.cloned.1.call-start = ((), (), s32[]{:S(2)}) async-start(), calls=%async_computation.1 | async-start | bytes 524288 | tf_op jit(solution)/shard_map/while/body/eval_jaxpr/psum | solution.py:60
  1208.5 25.4 %collective-permute-start = (bf16[1024,256]{1,0:T(8,128)(2,1)S(1)}, bf16[1024,256]{1,0:T(8,128)(2,1)S(1)}, u32[]{:S(2)}, u32[]{:S(2)}) collective-permute-start(bf16[1024,256]{1,0:T(8,128)(2,1)S(1)} %copy.14), channel_id=1, source_target_pairs={{448,0},{456,8},{464,16},{472,24},{480,32},{488,40},{496,48},{504,... | collective-permute-start | bytes 1572872 | tf_op jit(solution)/shard_map/while/body/eval_jaxpr/ppermute | solution.py:10
  1250.1 18.0 %collective-permute-start.6 = (bf16[2,128,256]{2,1,0:T(8,128)(2,1)S(1)}, bf16[2,128,256]{2,1,0:T(8,128)(2,1)S(1)}, u32[]{:S(2)}, u32[]{:S(2)}) collective-permute-start(bf16[2,128,256]{2,1,0:T(8,128)(2,1)S(1)} %slice.47), channel_id=1, source_target_pairs={{16,0},{24,8},{32,16},{40,24},{48,32},{56,40},{64,48},{72,56},{80,... | collective-permute-start | bytes 393224 | tf_op jit(solution)/shard_map/ppermute | solution.py:10
  (11 other events, 450.8 us)
Sparse Core Ops, SparseCore 0:
  10.1 303.2 all-gather.1
  357.3 68.5 all-reduce.2
  461.4 75.5 all-reduce.2
  572.1 75.5 all-reduce.2
  682.8 75.5 all-reduce.2
  793.6 75.5 all-reduce.2
  904.6 75.5 all-reduce.2
  1015.6 75.5 all-reduce.2
  1126.6 75.5 all-reduce.2
where the time goes:
time: 1290 us; the launch traced here: 1280 us
  waiting for transfers between devices  1120 us (87%)
  starting transfers between devices  87.7 us (7%)
  matrix products  33.5 us (3%)
  other arithmetic  30.5 us (2%)
  between operations  14.5 us (1%)
    psum x8, waiting for transfers between devices, one_turn(): lax.psum(inner_rows(queries, passage_block).astype(jnp.bfloat16), 'mp')  618 us
    all_gather x1, waiting for transfers between devices, per_device(): piece = lax.all_gather(proj_weight, 'dp', axis=0, tiled=True)  305 us
    ppermute x22, waiting for transfers between devices, shifted(): return lax.ppermute(block, axis, route)  193 us
    ppermute x22, starting transfers between devices, shifted(): return lax.ppermute(block, axis, route)  87.6 us
  transfers between devices with their start and end apart: 31, of which 31 were waited for; matrix products, arithmetic and copies ran while one was open for 2% of the time, Pallas kernels for 0%

commit v1 on v0

v1 whole, which is shorter than its diff:
```python
import jax
import jax.numpy as jnp
from jax import lax
from jax.sharding import Mesh, PartitionSpec as P

BF16 = jnp.bfloat16
F32 = jnp.float32
DP = ("x", "zl", "y")
MP = ("zh", "core")


def exchange(pieces, axes):
    return lax.all_to_all(pieces, axes, 0, 0, tiled=True)


def dot(left, right, contract):
    return lax.dot_general(left, right, (contract, ((), ())), preferred_element_type=F32)


def per_device(query_states, passage_states, proj_weight, positive_index, logit_scale, logit_bias):
    nx, nzl, ny, nzh = (lax.axis_size(a) for a in ("x", "zl", "y", "zh"))
    rows = query_states.shape[0]
    depth, cols = proj_weight.shape
    blocks = nzl * ny
    sub = rows // nzh
    scale_value = logit_scale[0]
    bias_value = logit_bias[0]

    w_all = exchange(jnp.broadcast_to(proj_weight[None], (nx * blocks, depth, cols)), DP)
    w_all = w_all.reshape(nx * blocks * depth, cols)
    passages = dot(passage_states, w_all, ((1,), (0,))).astype(BF16)
    queries = dot(query_states, w_all, ((1,), (0,))).astype(BF16)

    p_send = jnp.broadcast_to(passages.reshape(1, nzh, sub, cols), (blocks, nzh, sub, cols))
    p_tile = exchange(p_send.reshape(blocks * nzh, sub, cols), ("zl", "y", "zh"))
    p_tile = p_tile.reshape(blocks, nzh, sub, cols).transpose(0, 2, 1, 3)
    p_tile = p_tile.reshape(blocks * sub, nzh * cols)

    q_tile = exchange(jnp.broadcast_to(queries[None], (nzh, rows, cols)), "zh")
    q_tile = q_tile.transpose(1, 0, 2).reshape(rows, nzh * cols)
    q_tile = lax.all_gather(q_tile, "x", axis=0, tiled=True)

    part = dot(q_tile, p_tile, ((1,), (1,))).astype(BF16)
    other = lax.ppermute(part, "core", [(0, 1), (1, 0)])
    scores = part.astype(F32) + other.astype(F32)

    own_block = lax.axis_index("zl") * ny + lax.axis_index("y")
    place = positive_index - lax.axis_index("zh") * sub
    target = jnp.where((place >= 0) & (place < sub), own_block * sub + place, -1)
    own_x = jnp.arange(nx, dtype=jnp.int32)[:, None] == lax.axis_index("x")
    target = jnp.where(own_x, target[None, :], -1).reshape(nx * rows, 1)
    labels = (jnp.arange(blocks * sub, dtype=jnp.int32)[None, :] == target).astype(F32)
    logits = scale_value * scores + bias_value
    weight = (jax.nn.sigmoid(logits) - labels).astype(BF16)

    gp = dot(weight, q_tile, ((0,), (0,))).astype(BF16)
    gq = dot(weight, p_tile, ((1,), (0,))).astype(BF16)

    gp = gp.reshape(blocks, sub, nzh, cols).transpose(0, 2, 1, 3).reshape(blocks * nzh, sub, cols)
    gp = exchange(gp, ("zl", "y", "zh")).reshape(blocks, nzh, sub, cols)
    grad_p = jnp.sum(gp.astype(F32), axis=0).reshape(rows, cols)

    gq = exchange(gq, "x").reshape(nx, rows, nzh * cols)
    gq = jnp.sum(gq.astype(F32), axis=0).astype(BF16)
    gq = exchange(gq.reshape(rows, nzh, cols).transpose(1, 0, 2), "zh")
    grad_q = jnp.sum(gq.astype(F32), axis=0)
    return (scale_value * grad_q, scale_value * grad_p)


def solution(mesh):
    fine = Mesh(mesh.devices.reshape(4, 2, 8, 4, 2), DP + MP)
    in_specs = (P(DP, None), P(DP, None), P(DP, MP), P(DP), P(), P())
    out_specs = (P(DP, MP), P(DP, MP))
    return jax.shard_map(
        per_device, mesh=fine, in_specs=in_specs, out_specs=out_specs, check_vma=False
    )
```

time: 1290 us -> 198 us (0.15)
  the two profiles are of different devices: /device:TPU:128 before, /device:TPU:8 now
where the time goes in v1:
time: 198 us
  waiting for transfers between devices  74.5 us (38%)
  blocking collectives  60.6 us (31%)
  starting transfers between devices  32.5 us (16%)
  between operations  15.5 us (8%)
  local copies, waits for them, and re-layouts  7.01 us (4%)
  matrix products  5.76 us (3%)
    all_to_all x4, waiting for transfers between devices, exchange(): return lax.all_to_all(pieces, axes, 0, 0, tiled=True)  67.8 us
    all_to_all x2, blocking collectives, exchange(): return lax.all_to_all(pieces, axes, 0, 0, tiled=True)  60.6 us
    all_to_all x4, starting transfers between devices, exchange(): return lax.all_to_all(pieces, axes, 0, 0, tiled=True)  30.5 us
    dot_general x5, matrix products, dot(): lax.dot_general(left, right, (contract, ((), ())), preferred_element_type...  5.76 us
    all_gather x1, waiting for transfers between devices, per_device(): q_tile = lax.all_gather(q_tile, 'x', axis=0, tiled=True)  4.26 us
  transfers between devices with their start and end apart: 6, of which 6 were waited for; matrix products, arithmetic and copies ran while one was open for 3% of the time, Pallas kernels for 0%

profile of v1, /device:TPU:8, one launch (start us, length us, event | category | flops | bytes accessed | tf_op | source)
XLA Modules:
  0.0 197.7 jit_solution(11681373747413559871)
XLA Ops:
  7.2 0.9 broadcast_in_dim.46
  8.1 41.4 %all_to_all.34 = bf16[64,32,256]{2,1,0:T(8,128)(2,1)S(1)} all-to-all(bf16[64,32,256]{2,1,0:T(8,128)(2,1)S(1)} %broadcast_in_dim.46), channel_id=1, replica_groups=mesh['x'=4,'zl'=2,'y'=8,'zh'=4,'core'=2] {'x','zl','y'}, dimensions={0} | all-to-all | bytes 2097152 | tf_op jit(solution)/shard_map/all_to_all | solution.py:13
  49.9 0.7 broadcast_in_dim.47
  50.7 9.4 %all-to-all-start.1 = ((bf16[4,128,256]{1,2,0:T(8,128)(2,1)}), bf16[4,128,256]{1,2,0:T(8,128)(2,1)S(1)}, u32[]{:S(2)}, u32[]{:S(2)}) async-start(bf16[4,128,256]{1,2,0:T(8,128)(2,1)} %broadcast_in_dim.47), calls=%async_computation.1 | async-start | bytes 524288 | tf_op jit(solution)/shard_map/all_to_all | solution.py:13
  60.4 9.6 %all-to-all-done.1 = bf16[4,128,256]{1,2,0:T(8,128)(2,1)S(1)} async-done(((bf16[4,128,256]{1,2,0:T(8,128)(2,1)}), bf16[4,128,256]{1,2,0:T(8,128)(2,1)S(1)}, u32[]{:S(2)}, u32[]{:S(2)}) %all-to-all-start.1) | async-done | bytes 262176 | tf_op jit(solution)/shard_map/all_to_all | solution.py:13
  70.0 1.1 broadcast_in_dim.49
  71.1 5.6 %all-to-all-start.2 = ((bf16[64,32,256]{2,1,0:T(8,128)(2,1)}), bf16[64,32,256]{2,1,0:T(8,128)(2,1)S(1)}, u32[]{:S(2)}, u32[]{:S(2)}) async-start(bf16[64,32,256]{2,1,0:T(8,128)(2,1)} %bitcast.5), calls=%async_computation.2 | async-start | bytes 2097152 | tf_op jit(solution)/shard_map/all_to_all | solution.py:13
  76.8 0.7 all-gather.2.cloned.1.call-update
  78.8 25.6 %all-to-all-done.2 = bf16[64,32,256]{2,1,0:T(8,128)(2,1)S(1)} async-done(((bf16[64,32,256]{2,1,0:T(8,128)(2,1)}), bf16[64,32,256]{2,1,0:T(8,128)(2,1)S(1)}, u32[]{:S(2)}, u32[]{:S(2)}) %all-to-all-start.2) | async-done | bytes 1048608 | tf_op jit(solution)/shard_map/all_to_all | solution.py:13
  104.4 0.9 copy.21
  105.5 4.3 %all-gather.2.cloned.1.call-done = bf16[512,1024]{0,1:T(8,128)(2,1)} async-done(((bf16[128,1024]{0,1:T(8,128)(2,1)}), bf16[512,1024]{0,1:T(8,128)(2,1)}) %all-gather.2.cloned.1.call-update) | async-done | bytes 1048592 | tf_op jit(solution)/shard_map/all_gather | solution.py:41
  109.8 2.0 %convolution_convert_fusion.2 = bf16[512,512]{1,0:T(8,128)(2,1)S(1)} fusion(bf16[512,1024]{0,1:T(8,128)(2,1)} %all-gather.2.cloned.1.call-done, bf16[512,1024]{1,0:T(8,128)(2,1)S(1)} %bitcast.45), kind=kOutput, calls=%fused_computation.3 | convolution fusion | flops 537133056 | bytes 2621440 | tf_op jit(solution)/shard_map/dot_general | solution.py:17
  111.8 1.9 collective-permute-start
  113.8 1.8 collective-permute-done
  115.6 1.0 convolution_convert_fusion.1
  116.6 19.2 %all_to_all.35 = bf16[4,128,1024]{2,1,0:T(8,128)(2,1)S(1)} all-to-all(bf16[4,128,1024]{2,1,0:T(8,128)(2,1)S(1)} %bitcast.47), channel_id=1, replica_groups=mesh['x'=4,'zl'=2,'y'=8,'zh'=4,'core'=2] {'x'}, dimensions={0} | all-to-all | bytes 2097152 | tf_op jit(solution)/shard_map/all_to_all | solution.py:13
  136.2 0.8 copy.23
  137.0 7.4 %all-to-all-start.4 = ((bf16[4,128,256]{2,1,0:T(8,128)(2,1)}), bf16[4,128,256]{2,1,0:T(8,128)(2,1)S(1)}, u32[]{:S(2)}, u32[]{:S(2)}) async-start(bf16[4,128,256]{2,1,0:T(8,128)(2,1)} %copy.23), calls=%async_computation.4 | async-start | bytes 524288 | tf_op jit(solution)/shard_map/all_to_all | solution.py:13
  144.4 2.1 %convolution_convert_fusion = bf16[512,1024]{1,0:T(8,128)(2,1)S(1)} fusion(bf16[512,1024]{0,1:T(8,128)(2,1)S(1)} %copy-done.4, bf16[512,512]{1,0:T(8,128)(2,1)} %copy-done.5, bf16[512,512]{1,0:T(8,128)(2,1)S(1)} %convolution_convert_fusion.2, s32[512]{0:T(512)S(1)} %select_bitcast_fusion, f32[]{:T(128)} %bitcast.39, f32[]{:T(128)} %bitcast.37), kind=kOutput, calls=%fused_computation.1 | convolution fusion | flops 540540928 | bytes 3147784 | tf_op jit(solution)/shard_map/dot_general | solution.py:17
  146.6 0.8 reshape.70
  147.4 1.2 copy.24
  148.5 6.5 %all-to-all-done.4 = bf16[4,128,256]{2,1,0:T(8,128)(2,1)S(1)} async-done(((bf16[4,128,256]{2,1,0:T(8,128)(2,1)}), bf16[4,128,256]{2,1,0:T(8,128)(2,1)S(1)}, u32[]{:S(2)}, u32[]{:S(2)}) %all-to-all-start.4) | async-done | bytes 262176 | tf_op jit(solution)/shard_map/all_to_all | solution.py:13
  155.0 8.1 %all-to-all-start.5 = ((bf16[64,32,256]{2,1,0:T(8,128)(2,1)}), bf16[64,32,256]{2,1,0:T(8,128)(2,1)S(1)}, u32[]{:S(2)}, u32[]{:S(2)}) async-start(bf16[64,32,256]{2,1,0:T(8,128)(2,1)} %bitcast.14), calls=%async_computation.5 | async-start | bytes 2097152 | tf_op jit(solution)/shard_map/all_to_all | solution.py:13
  163.8 26.2 %all-to-all-done.5 = bf16[64,32,256]{2,1,0:T(8,128)(2,1)S(1)} async-done(((bf16[64,32,256]{2,1,0:T(8,128)(2,1)}), bf16[64,32,256]{2,1,0:T(8,128)(2,1)S(1)}, u32[]{:S(2)}, u32[]{:S(2)}) %all-to-all-start.5) | async-done | bytes 1048608 | tf_op jit(solution)/shard_map/all_to_all | solution.py:13
  (26 shorter events, 3.0 us)
Async XLA Ops:
  7.2 42.3 %copy-start = (bf16[128,2048]{1,0:T(8,128)(2,1)S(1)}, bf16[128,2048]{1,0:T(8,128)(2,1)}, u32[]{:S(2)}) copy-start(bf16[128,2048]{1,0:T(8,128)(2,1)} %param.6) | copy-start | bytes 1572868
  49.5 10.6 %copy-start.2 = (bf16[128,2048]{1,0:T(8,128)(2,1)S(1)}, bf16[128,2048]{1,0:T(8,128)(2,1)}, u32[]{:S(2)}) copy-start(bf16[128,2048]{1,0:T(8,128)(2,1)} %param.7) | copy-start | bytes 1572868
  50.7 19.3 %all-to-all-start.1 = ((bf16[4,128,256]{1,2,0:T(8,128)(2,1)}), bf16[4,128,256]{1,2,0:T(8,128)(2,1)S(1)}, u32[]{:S(2)}, u32[]{:S(2)}) async-start(bf16[4,128,256]{1,2,0:T(8,128)(2,1)} %broadcast_in_dim.47), calls=%async_computation.1 | async-start | bytes 524288 | tf_op jit(solution)/shard_map/all_to_all | solution.py:13
  70.0 1.2 copy-start.1
  71.1 33.3 %all-to-all-start.2 = ((bf16[64,32,256]{2,1,0:T(8,128)(2,1)}), bf16[64,32,256]{2,1,0:T(8,128)(2,1)S(1)}, u32[]{:S(2)}, u32[]{:S(2)}) async-start(bf16[64,32,256]{2,1,0:T(8,128)(2,1)} %bitcast.5), calls=%async_computation.2 | async-start | bytes 2097152 | tf_op jit(solution)/shard_map/all_to_all | solution.py:13
  76.8 33.0 %all-gather.2.cloned.1.call-start = ((), (), s32[]{:S(2)}) async-start(), calls=%async_computation.6 | async-start | bytes 1310720 | tf_op jit(solution)/shard_map/all_gather | solution.py:41
  109.8 4.0 %copy-start.3 = (s32[128]{0:T(128)S(1)}, s32[128]{0:T(128)}, u32[]{:S(2)}) copy-start(s32[128]{0:T(128)} %param.9) | copy-start | bytes 1540
  111.8 3.8 %collective-permute-start = (bf16[512,512]{1,0:T(8,128)(2,1)S(1)}, bf16[512,512]{1,0:T(8,128)(2,1)S(1)}, u32[]{:S(2)}, u32[]{:S(2)}) collective-permute-start(bf16[512,512]{1,0:T(8,128)(2,1)S(1)} %convolution_convert_fusion.2), channel_id=1, source_target_pairs={{0,1},{1,0},{2,3},{3,2},{4,5},{5,4},{6,7},{7,6},{8,9},{9,8},{10,11... | collective-permute-start | bytes 1572872 | tf_op jit(solution)/shard_map/ppermute | solution.py:44
  115.6 1.0 copy-start.5
  136.2 8.2 %copy-start.4 = (bf16[512,1024]{0,1:T(8,128)(2,1)S(1)}, bf16[512,1024]{0,1:T(8,128)(2,1)}, u32[]{:S(2)}) copy-start(bf16[512,1024]{0,1:T(8,128)(2,1)} %all-gather.2.cloned.1.call-done) | copy-start | bytes 3145732
  137.0 18.0 %all-to-all-start.4 = ((bf16[4,128,256]{2,1,0:T(8,128)(2,1)}), bf16[4,128,256]{2,1,0:T(8,128)(2,1)S(1)}, u32[]{:S(2)}, u32[]{:S(2)}) async-start(bf16[4,128,256]{2,1,0:T(8,128)(2,1)} %copy.23), calls=%async_computation.4 | async-start | bytes 524288 | tf_op jit(solution)/shard_map/all_to_all | solution.py:13
  155.0 35.0 %all-to-all-start.5 = ((bf16[64,32,256]{2,1,0:T(8,128)(2,1)}), bf16[64,32,256]{2,1,0:T(8,128)(2,1)S(1)}, u32[]{:S(2)}, u32[]{:S(2)}) async-start(bf16[64,32,256]{2,1,0:T(8,128)(2,1)} %bitcast.14), calls=%async_computation.5 | async-start | bytes 2097152 | tf_op jit(solution)/shard_map/all_to_all | solution.py:13
Sparse Core Ops, SparseCore 0:
  79.7 30.0 all-gather.1

commit v2 on v1

--- a/solution.py
+++ b/solution.py
@@ -17,8 +17,14 @@
     return lax.dot_general(left, right, (contract, ((), ())), preferred_element_type=F32)
 
 
+def shifted(block, axis, step):
+    size = lax.axis_size(axis)
+    return lax.ppermute(block, axis, [(i, (i + step) % size) for i in range(size)])
+
+
 def per_device(query_states, passage_states, proj_weight, positive_index, logit_scale, logit_bias):
     nx, nzl, ny, nzh = (lax.axis_size(a) for a in ("x", "zl", "y", "zh"))
+    zh = lax.axis_index("zh")
     rows = query_states.shape[0]
     depth, cols = proj_weight.shape
     blocks = nzl * ny
@@ -36,34 +42,41 @@
     p_tile = p_tile.reshape(blocks, nzh, sub, cols).transpose(0, 2, 1, 3)
     p_tile = p_tile.reshape(blocks * sub, nzh * cols)
 
-    q_tile = exchange(jnp.broadcast_to(queries[None], (nzh, rows, cols)), "zh")
-    q_tile = q_tile.transpose(1, 0, 2).reshape(rows, nzh * cols)
-    q_tile = lax.all_gather(q_tile, "x", axis=0, tiled=True)
+    held = jnp.stack([queries] + [shifted(queries, "zh", k) for k in range(1, nzh)])
+    ordered = [lax.dynamic_index_in_dim(held, (zh - j) % nzh, 0, False) for j in range(nzh)]
+    q_own = jnp.concatenate(ordered, axis=1)
+    q_tile = jnp.concatenate([q_own] + [shifted(q_own, "x", k) for k in range(1, nx)], axis=0)
 
     part = dot(q_tile, p_tile, ((1,), (1,))).astype(BF16)
     other = lax.ppermute(part, "core", [(0, 1), (1, 0)])
     scores = part.astype(F32) + other.astype(F32)
 
     own_block = lax.axis_index("zl") * ny + lax.axis_index("y")
-    place = positive_index - lax.axis_index("zh") * sub
+    place = positive_index - zh * sub
     target = jnp.where((place >= 0) & (place < sub), own_block * sub + place, -1)
-    own_x = jnp.arange(nx, dtype=jnp.int32)[:, None] == lax.axis_index("x")
-    target = jnp.where(own_x, target[None, :], -1).reshape(nx * rows, 1)
+    target = jnp.pad(target, (0, (nx - 1) * rows), constant_values=-1)[:, None]
     labels = (jnp.arange(blocks * sub, dtype=jnp.int32)[None, :] == target).astype(F32)
     logits = scale_value * scores + bias_value
     weight = (jax.nn.sigmoid(logits) - labels).astype(BF16)
 
     gp = dot(weight, q_tile, ((0,), (0,))).astype(BF16)
-    gq = dot(weight, p_tile, ((1,), (0,))).astype(BF16)
-
     gp = gp.reshape(blocks, sub, nzh, cols).transpose(0, 2, 1, 3).reshape(blocks * nzh, sub, cols)
     gp = exchange(gp, ("zl", "y", "zh")).reshape(blocks, nzh, sub, cols)
     grad_p = jnp.sum(gp.astype(F32), axis=0).reshape(rows, cols)
 
-    gq = exchange(gq, "x").reshape(nx, rows, nzh * cols)
-    gq = jnp.sum(gq.astype(F32), axis=0).astype(BF16)
-    gq = exchange(gq.reshape(rows, nzh, cols).transpose(1, 0, 2), "zh")
-    grad_q = jnp.sum(gq.astype(F32), axis=0)
+    gq = dot(weight, p_tile, ((1,), (0,)))
+    back = [
+        shifted(gq[k * rows : (k + 1) * rows].astype(BF16), "x", -k).astype(F32)
+        for k in range(1, nx)
+    ]
+    own = gq[:rows] + sum(back)
+
+    def feature_block(j):
+        return lax.dynamic_slice_in_dim(own, (j % nzh) * cols, cols, 1)
+
+    grad_q = feature_block(zh) + sum(
+        shifted(feature_block(zh + k).astype(BF16), "zh", k).astype(F32) for k in range(1, nzh)
+    )
     return (scale_value * grad_q, scale_value * grad_p)
 
 

time: 198 us -> 176 us (0.89)
  the two profiles are of different devices: /device:TPU:8 before, /device:TPU:1 now
where the time goes in v2:
time: 176 us; the launch traced here: 175 us
  starting transfers between devices  72 us (41%)
  waiting for transfers between devices  42.7 us (24%)
  blocking collectives  39.3 us (22%)
  matrix products  8.82 us (5%)
  local copies, waits for them, and re-layouts  7.12 us (4%)
  other arithmetic  2.78 us (2%)
  between operations  2.36 us (1%)
    ppermute x12, starting transfers between devices, shifted(): lax.ppermute(block, axis, [(i, (i + step) % size) for i in range(size)])  45.8 us
    ppermute x12, waiting for transfers between devices, shifted(): lax.ppermute(block, axis, [(i, (i + step) % size) for i in range(size)])  42.5 us
    all_to_all x1, blocking collectives, exchange(): return lax.all_to_all(pieces, axes, 0, 0, tiled=True)  39.3 us
    all_to_all x2, starting transfers between devices, exchange(): return lax.all_to_all(pieces, axes, 0, 0, tiled=True)  21.9 us
    dot_general x5, matrix products, dot(): lax.dot_general(left, right, (contract, ((), ())), preferred_element_type...  8.82 us
    ppermute x1, starting transfers between devices, per_device(): other = lax.ppermute(part, 'core', [(0, 1), (1, 0)])  4.27 us
  transfers between devices with their start and end apart: 15, of which 10 were waited for; matrix products, arithmetic and copies ran while one was open for 4% of the time, Pallas kernels for 0%

profile of v2, /device:TPU:1, one launch (start us, length us, event | category | flops | bytes accessed | tf_op | source)
XLA Modules:
  0.0 175.0 jit_solution(5098232395876624536)
XLA Ops:
  1.5 39.3 %all_to_all.15 = bf16[64,32,256]{2,1,0:T(8,128)(2,1)S(1)} all-to-all(bf16[64,32,256]{2,1,0:T(8,128)(2,1)S(1)} %broadcast_in_dim.10), channel_id=1, replica_groups=mesh['x'=4,'zl'=2,'y'=8,'zh'=4,'core'=2] {'x','zl','y'}, dimensions={0} | all-to-all | bytes 2097152 | tf_op jit(solution)/shard_map/all_to_all | solution.py:13
  42.2 13.4 %all-to-all-start.1 = ((bf16[64,32,256]{2,1,0:T(8,128)(2,1)}), bf16[64,32,256]{2,1,0:T(8,128)(2,1)S(1)}, u32[]{:S(2)}, u32[]{:S(2)}) async-start(bf16[64,32,256]{2,1,0:T(8,128)(2,1)} %bitcast.45), calls=%async_computation.1 | async-start | bytes 2097152 | tf_op jit(solution)/shard_map/all_to_all | solution.py:13
  56.0 3.8 %collective-permute-start = (bf16[128,256]{1,0:T(8,128)(2,1)S(1)}, bf16[128,256]{1,0:T(8,128)(2,1)S(1)}, u32[]{:S(2)}, u32[]{:S(2)}) collective-permute-start(bf16[128,256]{1,0:T(8,128)(2,1)S(1)} %convolution_convert_fusion.3), channel_id=1, source_target_pairs={{0,2},{2,4},{4,6},{6,0},{1,3},{3,5},{5,7},{7,1},{8,10},{10,12},{12... | collective-permute-start | bytes 196616 | tf_op jit(solution)/shard_map/ppermute | solution.py:22
  59.8 5.2 %collective-permute-start.1 = (bf16[128,256]{1,0:T(8,128)(2,1)S(1)}, bf16[128,256]{1,0:T(8,128)(2,1)S(1)}, u32[]{:S(2)}, u32[]{:S(2)}) collective-permute-start(bf16[128,256]{1,0:T(8,128)(2,1)S(1)} %convolution_convert_fusion.3), channel_id=1, source_target_pairs={{0,4},{2,6},{4,0},{6,2},{1,5},{3,7},{5,1},{7,3},{8,12},{10,14},{12... | collective-permute-start | bytes 196616 | tf_op jit(solution)/shard_map/ppermute | solution.py:22
  65.0 5.2 %collective-permute-start.2 = (bf16[128,256]{1,0:T(8,128)(2,1)S(1)}, bf16[128,256]{1,0:T(8,128)(2,1)S(1)}, u32[]{:S(2)}, u32[]{:S(2)}) collective-permute-start(bf16[128,256]{1,0:T(8,128)(2,1)S(1)} %convolution_convert_fusion.3), channel_id=1, source_target_pairs={{0,6},{2,0},{4,2},{6,4},{1,7},{3,1},{5,3},{7,5},{8,14},{10,8},{12,... | collective-permute-start | bytes 196616 | tf_op jit(solution)/shard_map/ppermute | solution.py:22
  70.3 14.0 %collective-permute-done = bf16[128,256]{1,0:T(8,128)(2,1)S(1)} collective-permute-done((bf16[128,256]{1,0:T(8,128)(2,1)S(1)}, bf16[128,256]{1,0:T(8,128)(2,1)S(1)}, u32[]{:S(2)}, u32[]{:S(2)}) %collective-permute-start) | collective-permute-done | bytes 65568 | tf_op jit(solution)/shard_map/ppermute | solution.py:22
  84.3 4.3 %collective-permute-done.1 = bf16[128,256]{1,0:T(8,128)(2,1)S(1)} collective-permute-done((bf16[128,256]{1,0:T(8,128)(2,1)S(1)}, bf16[128,256]{1,0:T(8,128)(2,1)S(1)}, u32[]{:S(2)}, u32[]{:S(2)}) %collective-permute-start.1) | collective-permute-done | bytes 65568 | tf_op jit(solution)/shard_map/ppermute | solution.py:22
  90.6 3.4 %collective-permute-start.4 = (bf16[128,1024]{1,0:T(8,128)(2,1)S(1)}, bf16[128,1024]{1,0:T(8,128)(2,1)}, u32[]{:S(2)}, u32[]{:S(2)}) collective-permute-start(bf16[128,1024]{1,0:T(8,128)(2,1)S(1)} %pad_maximum_fusion.2), channel_id=1, source_target_pairs={{0,256},{128,384},{256,0},{384,128},{1,257},{129,385},{257,1},{385... | collective-permute-start | bytes 786440 | tf_op jit(solution)/shard_map/ppermute | solution.py:22
  94.1 3.4 %collective-permute-start.5 = (bf16[128,1024]{1,0:T(8,128)(2,1)S(1)}, bf16[128,1024]{1,0:T(8,128)(2,1)}, u32[]{:S(2)}, u32[]{:S(2)}) collective-permute-start(bf16[128,1024]{1,0:T(8,128)(2,1)S(1)} %pad_maximum_fusion.2), channel_id=1, source_target_pairs={{0,384},{128,0},{256,128},{384,256},{1,385},{129,1},{257,129},{385... | collective-permute-start | bytes 786440 | tf_op jit(solution)/shard_map/ppermute | solution.py:22
  99.2 3.4 %collective-permute-done.4 = bf16[128,1024]{1,0:T(8,128)(2,1)} collective-permute-done((bf16[128,1024]{1,0:T(8,128)(2,1)S(1)}, bf16[128,1024]{1,0:T(8,128)(2,1)}, u32[]{:S(2)}, u32[]{:S(2)}) %collective-permute-start.4) | collective-permute-done | bytes 262176 | tf_op jit(solution)/shard_map/ppermute | solution.py:22
  102.5 3.9 %collective-permute-done.5 = bf16[128,1024]{1,0:T(8,128)(2,1)} collective-permute-done((bf16[128,1024]{1,0:T(8,128)(2,1)S(1)}, bf16[128,1024]{1,0:T(8,128)(2,1)}, u32[]{:S(2)}, u32[]{:S(2)}) %collective-permute-start.5) | collective-permute-done | bytes 262176 | tf_op jit(solution)/shard_map/ppermute | solution.py:22
  108.3 4.3 %collective-permute-start.6 = (bf16[512,512]{1,0:T(8,128)(2,1)S(1)}, bf16[512,512]{1,0:T(8,128)(2,1)S(1)}, u32[]{:S(2)}, u32[]{:S(2)}) collective-permute-start(bf16[512,512]{1,0:T(8,128)(2,1)S(1)} %convolution_convert_fusion.1), channel_id=1, source_target_pairs={{0,1},{1,0},{2,3},{3,2},{4,5},{5,4},{6,7},{7,6},{8,9},{9,8},{10,11... | collective-permute-start | bytes 1572872 | tf_op jit(solution)/shard_map/ppermute | solution.py:51
  114.9 2.9 %convolution_convert_fusion = bf16[512,1024]{1,0:T(8,128)(2,1)} fusion(bf16[128,1024]{1,0:T(8,128)(2,1)} %collective-permute-done.5, bf16[128,1024]{1,0:T(8,128)(2,1)} %collective-permute-done.4, bf16[128,1024]{1,0:T(8,128)(2,1)S(1)} %copy-done.5, bf16[128,256]{1,0:T(8,128)(2,1)S(1)} %get-tuple-element.9, bf16[128,256]{1,0:T(8,128)(2,1)S(1)} %get-tuple-element.10, ...), kind=kOutput, calls=%fused_computation.1 | convolution fusion | flops 547880960 | bytes 3147784 | tf_op jit(solution)/shard_map/dot_general | solution.py:17
  120.9 8.5 %all-to-all-start.2 = ((bf16[64,32,256]{2,1,0:T(8,128)(2,1)}), bf16[64,32,256]{2,1,0:T(8,128)(2,1)S(1)}, u32[]{:S(2)}, u32[]{:S(2)}) async-start(bf16[64,32,256]{2,1,0:T(8,128)(2,1)} %bitcast.16), calls=%async_computation.2 | async-start | bytes 2097152 | tf_op jit(solution)/shard_map/all_to_all | solution.py:13
  129.4 3.4 %fusion.2 = (bf16[512,1024]{1,0:T(8,128)(2,1)S(1)}, f32[512,1024]{1,0:T(8,128)}) fusion(bf16[512,1024]{1,0:T(8,128)(2,1)S(1)} %bitcast.48, bf16[512,512]{1,0:T(8,128)(2,1)} %copy-done.3, bf16[512,512]{1,0:T(8,128)(2,1)S(1)} %convolution_convert_fusion.1, s32[512]{0:T(512)S(1)} %pad.4, f32[]{:T(128)} %bitcast.39, f32[]{:T(128)} %bitcast.36), kind=kOutput, calls=%fused_computation.23 | convolution fusion | flops 540540928 | bytes 5244936 | tf_op jit(solution)/shard_map/dot_general | solution.py:17
  132.8 4.3 %collective-permute-start.7 = (bf16[128,1024]{1,0:T(8,128)(2,1)S(1)}, bf16[128,1024]{1,0:T(8,128)(2,1)S(1)}, u32[]{:S(2)}, u32[]{:S(2)}) collective-permute-start(bf16[128,1024]{1,0:T(8,128)(2,1)S(1)} %get-tuple-element.2), channel_id=1, source_target_pairs={{0,384},{128,0},{256,128},{384,256},{1,385},{129,1},{257,129},{385... | collective-permute-start | bytes 786440 | tf_op jit(solution)/shard_map/ppermute | solution.py:22
  137.1 1.9 %collective-permute-start.8 = (bf16[128,1024]{1,0:T(8,128)(2,1)S(1)}, bf16[128,1024]{1,0:T(8,128)(2,1)S(1)}, u32[]{:S(2)}, u32[]{:S(2)}) collective-permute-start(bf16[128,1024]{1,0:T(8,128)(2,1)S(1)} %get-tuple-element.4), channel_id=1, source_target_pairs={{0,256},{128,384},{256,0},{384,128},{1,257},{129,385},{257,1},{385... | collective-permute-start | bytes 786440 | tf_op jit(solution)/shard_map/ppermute | solution.py:22
  139.1 2.5 %collective-permute-start.9 = (bf16[128,1024]{1,0:T(8,128)(2,1)S(1)}, bf16[128,1024]{1,0:T(8,128)(2,1)S(1)}, u32[]{:S(2)}, u32[]{:S(2)}) collective-permute-start(bf16[128,1024]{1,0:T(8,128)(2,1)S(1)} %get-tuple-element.3), channel_id=1, source_target_pairs={{0,128},{128,256},{256,384},{384,0},{1,129},{129,257},{257,385},{3... | collective-permute-start | bytes 786440 | tf_op jit(solution)/shard_map/ppermute | solution.py:22
  142.7 4.7 %collective-permute-done.8 = bf16[128,1024]{1,0:T(8,128)(2,1)S(1)} collective-permute-done((bf16[128,1024]{1,0:T(8,128)(2,1)S(1)}, bf16[128,1024]{1,0:T(8,128)(2,1)S(1)}, u32[]{:S(2)}, u32[]{:S(2)}) %collective-permute-start.8) | collective-permute-done | bytes 262176 | tf_op jit(solution)/shard_map/ppermute | solution.py:22
  147.4 6.9 %collective-permute-done.9 = bf16[128,1024]{1,0:T(8,128)(2,1)S(1)} collective-permute-done((bf16[128,1024]{1,0:T(8,128)(2,1)S(1)}, bf16[128,1024]{1,0:T(8,128)(2,1)S(1)}, u32[]{:S(2)}, u32[]{:S(2)}) %collective-permute-start.9) | collective-permute-done | bytes 262176 | tf_op jit(solution)/shard_map/ppermute | solution.py:22
  155.6 3.8 %collective-permute-start.10 = (bf16[128,256]{1,0:T(8,128)(2,1)S(1)}, bf16[128,256]{1,0:T(8,128)(2,1)S(1)}, u32[]{:S(2)}, u32[]{:S(2)}) collective-permute-start(bf16[128,256]{1,0:T(8,128)(2,1)S(1)} %get-tuple-element.5), channel_id=1, source_target_pairs={{0,2},{2,4},{4,6},{6,0},{1,3},{3,5},{5,7},{7,1},{8,10},{10,12},{12... | collective-permute-start | bytes 196616 | tf_op jit(solution)/shard_map/ppermute | solution.py:22
  159.4 5.2 %collective-permute-start.11 = (bf16[128,256]{1,0:T(8,128)(2,1)S(1)}, bf16[128,256]{1,0:T(8,128)(2,1)S(1)}, u32[]{:S(2)}, u32[]{:S(2)}) collective-permute-start(bf16[128,256]{1,0:T(8,128)(2,1)S(1)} %get-tuple-element.7), channel_id=1, source_target_pairs={{0,4},{2,6},{4,0},{6,2},{1,5},{3,7},{5,1},{7,3},{8,12},{10,14},{12... | collective-permute-start | bytes 196616 | tf_op jit(solution)/shard_map/ppermute | solution.py:22
  164.6 5.2 %collective-permute-start.12 = (bf16[128,256]{1,0:T(8,128)(2,1)S(1)}, bf16[128,256]{1,0:T(8,128)(2,1)S(1)}, u32[]{:S(2)}, u32[]{:S(2)}) collective-permute-start(bf16[128,256]{1,0:T(8,128)(2,1)S(1)} %get-tuple-element.6), channel_id=1, source_target_pairs={{0,6},{2,0},{4,2},{6,4},{1,7},{3,1},{5,3},{7,5},{8,14},{10,8},{12,... | collective-permute-start | bytes 196616 | tf_op jit(solution)/shard_map/ppermute | solution.py:22
  169.8 3.6 %collective-permute-done.12 = bf16[128,256]{1,0:T(8,128)(2,1)S(1)} collective-permute-done((bf16[128,256]{1,0:T(8,128)(2,1)S(1)}, bf16[128,256]{1,0:T(8,128)(2,1)S(1)}, u32[]{:S(2)}, u32[]{:S(2)}) %collective-permute-start.12) | collective-permute-done | bytes 65568 | tf_op jit(solution)/shard_map/ppermute | solution.py:22
  (41 shorter events, 16.3 us)
Async XLA Ops:
  0.6 40.2 %copy-start = (bf16[128,2048]{1,0:T(8,128)(2,1)S(1)}, bf16[128,2048]{1,0:T(8,128)(2,1)}, u32[]{:S(2)}) copy-start(bf16[128,2048]{1,0:T(8,128)(2,1)} %param.7) | copy-start | bytes 1572868
  40.8 14.9 %copy-start.1 = (bf16[128,2048]{1,0:T(8,128)(2,1)S(1)}, bf16[128,2048]{1,0:T(8,128)(2,1)}, u32[]{:S(2)}) copy-start(bf16[128,2048]{1,0:T(8,128)(2,1)} %param.6) | copy-start | bytes 1572868
  42.2 55.2 %all-to-all-start.1 = ((bf16[64,32,256]{2,1,0:T(8,128)(2,1)}), bf16[64,32,256]{2,1,0:T(8,128)(2,1)S(1)}, u32[]{:S(2)}, u32[]{:S(2)}) async-start(bf16[64,32,256]{2,1,0:T(8,128)(2,1)} %bitcast.45), calls=%async_computation.1 | async-start | bytes 2097152 | tf_op jit(solution)/shard_map/all_to_all | solution.py:13
  56.0 28.3 %collective-permute-start = (bf16[128,256]{1,0:T(8,128)(2,1)S(1)}, bf16[128,256]{1,0:T(8,128)(2,1)S(1)}, u32[]{:S(2)}, u32[]{:S(2)}) collective-permute-start(bf16[128,256]{1,0:T(8,128)(2,1)S(1)} %convolution_convert_fusion.3), channel_id=1, source_target_pairs={{0,2},{2,4},{4,6},{6,0},{1,3},{3,5},{5,7},{7,1},{8,10},{10,12},{12... | collective-permute-start | bytes 196616 | tf_op jit(solution)/shard_map/ppermute | solution.py:22
  59.8 28.8 %collective-permute-start.1 = (bf16[128,256]{1,0:T(8,128)(2,1)S(1)}, bf16[128,256]{1,0:T(8,128)(2,1)S(1)}, u32[]{:S(2)}, u32[]{:S(2)}) collective-permute-start(bf16[128,256]{1,0:T(8,128)(2,1)S(1)} %convolution_convert_fusion.3), channel_id=1, source_target_pairs={{0,4},{2,6},{4,0},{6,2},{1,5},{3,7},{5,1},{7,3},{8,12},{10,14},{12... | collective-permute-start | bytes 196616 | tf_op jit(solution)/shard_map/ppermute | solution.py:22
  65.0 23.6 %collective-permute-start.2 = (bf16[128,256]{1,0:T(8,128)(2,1)S(1)}, bf16[128,256]{1,0:T(8,128)(2,1)S(1)}, u32[]{:S(2)}, u32[]{:S(2)}) collective-permute-start(bf16[128,256]{1,0:T(8,128)(2,1)S(1)} %convolution_convert_fusion.3), channel_id=1, source_target_pairs={{0,6},{2,0},{4,2},{6,4},{1,7},{3,1},{5,3},{7,5},{8,14},{10,8},{12,... | collective-permute-start | bytes 196616 | tf_op jit(solution)/shard_map/ppermute | solution.py:22
  88.7 10.5 %collective-permute-start.3 = (bf16[128,1024]{1,0:T(8,128)(2,1)S(1)}, bf16[128,1024]{1,0:T(8,128)(2,1)S(1)}, u32[]{:S(2)}, u32[]{:S(2)}) collective-permute-start(bf16[128,1024]{1,0:T(8,128)(2,1)S(1)} %pad_maximum_fusion.2), channel_id=1, source_target_pairs={{0,128},{128,256},{256,384},{384,0},{1,129},{129,257},{257,385},{3... | collective-permute-start | bytes 786440 | tf_op jit(solution)/shard_map/ppermute | solution.py:22
  90.6 11.9 %collective-permute-start.4 = (bf16[128,1024]{1,0:T(8,128)(2,1)S(1)}, bf16[128,1024]{1,0:T(8,128)(2,1)}, u32[]{:S(2)}, u32[]{:S(2)}) collective-permute-start(bf16[128,1024]{1,0:T(8,128)(2,1)S(1)} %pad_maximum_fusion.2), channel_id=1, source_target_pairs={{0,256},{128,384},{256,0},{384,128},{1,257},{129,385},{257,1},{385... | collective-permute-start | bytes 786440 | tf_op jit(solution)/shard_map/ppermute | solution.py:22
  94.1 12.3 %collective-permute-start.5 = (bf16[128,1024]{1,0:T(8,128)(2,1)S(1)}, bf16[128,1024]{1,0:T(8,128)(2,1)}, u32[]{:S(2)}, u32[]{:S(2)}) collective-permute-start(bf16[128,1024]{1,0:T(8,128)(2,1)S(1)} %pad_maximum_fusion.2), channel_id=1, source_target_pairs={{0,384},{128,0},{256,128},{384,256},{1,385},{129,1},{257,129},{385... | collective-permute-start | bytes 786440 | tf_op jit(solution)/shard_map/ppermute | solution.py:22
  99.2 7.2 %copy-start.4 = (bf16[128,1024]{1,0:T(8,128)(2,1)}, bf16[128,1024]{1,0:T(8,128)(2,1)S(1)}, u32[]{:S(2)}) copy-start(bf16[128,1024]{1,0:T(8,128)(2,1)S(1)} %collective-permute-done.3) | copy-start | bytes 786436
  106.4 6.2 %copy-start.2 = (s32[128]{0:T(128)S(1)}, s32[128]{0:T(128)}, u32[]{:S(2)}) copy-start(s32[128]{0:T(128)} %param.9) | copy-start | bytes 1540
  106.4 8.5 %copy-start.5 = (bf16[128,1024]{1,0:T(8,128)(2,1)S(1)}, bf16[128,1024]{1,0:T(8,128)(2,1)}, u32[]{:S(2)}) copy-start(bf16[128,1024]{1,0:T(8,128)(2,1)} %copy-done.4) | copy-start | bytes 786436
  108.3 5.8 %collective-permute-start.6 = (bf16[512,512]{1,0:T(8,128)(2,1)S(1)}, bf16[512,512]{1,0:T(8,128)(2,1)S(1)}, u32[]{:S(2)}, u32[]{:S(2)}) collective-permute-start(bf16[512,512]{1,0:T(8,128)(2,1)S(1)} %convolution_convert_fusion.1), channel_id=1, source_target_pairs={{0,1},{1,0},{2,3},{3,2},{4,5},{5,4},{6,7},{7,6},{8,9},{9,8},{10,11... | collective-permute-start | bytes 1572872 | tf_op jit(solution)/shard_map/ppermute | solution.py:51
  114.1 0.8 copy-start.3
  120.9 53.3 %all-to-all-start.2 = ((bf16[64,32,256]{2,1,0:T(8,128)(2,1)}), bf16[64,32,256]{2,1,0:T(8,128)(2,1)S(1)}, u32[]{:S(2)}, u32[]{:S(2)}) async-start(bf16[64,32,256]{2,1,0:T(8,128)(2,1)} %bitcast.16), calls=%async_computation.2 | async-start | bytes 2097152 | tf_op jit(solution)/shard_map/all_to_all | solution.py:13
  132.8 9.9 %collective-permute-start.7 = (bf16[128,1024]{1,0:T(8,128)(2,1)S(1)}, bf16[128,1024]{1,0:T(8,128)(2,1)S(1)}, u32[]{:S(2)}, u32[]{:S(2)}) collective-permute-start(bf16[128,1024]{1,0:T(8,128)(2,1)S(1)} %get-tuple-element.2), channel_id=1, source_target_pairs={{0,384},{128,0},{256,128},{384,256},{1,385},{129,1},{257,129},{385... | collective-permute-start | bytes 786440 | tf_op jit(solution)/shard_map/ppermute | solution.py:22
  137.1 10.3 %collective-permute-start.8 = (bf16[128,1024]{1,0:T(8,128)(2,1)S(1)}, bf16[128,1024]{1,0:T(8,128)(2,1)S(1)}, u32[]{:S(2)}, u32[]{:S(2)}) collective-permute-start(bf16[128,1024]{1,0:T(8,128)(2,1)S(1)} %get-tuple-element.4), channel_id=1, source_target_pairs={{0,256},{128,384},{256,0},{384,128},{1,257},{129,385},{257,1},{385... | collective-permute-start | bytes 786440 | tf_op jit(solution)/shard_map/ppermute | solution.py:22
  139.1 15.3 %collective-permute-start.9 = (bf16[128,1024]{1,0:T(8,128)(2,1)S(1)}, bf16[128,1024]{1,0:T(8,128)(2,1)S(1)}, u32[]{:S(2)}, u32[]{:S(2)}) collective-permute-start(bf16[128,1024]{1,0:T(8,128)(2,1)S(1)} %get-tuple-element.3), channel_id=1, source_target_pairs={{0,128},{128,256},{256,384},{384,0},{1,129},{129,257},{257,385},{3... | collective-permute-start | bytes 786440 | tf_op jit(solution)/shard_map/ppermute | solution.py:22
  155.6 14.3 %collective-permute-start.10 = (bf16[128,256]{1,0:T(8,128)(2,1)S(1)}, bf16[128,256]{1,0:T(8,128)(2,1)S(1)}, u32[]{:S(2)}, u32[]{:S(2)}) collective-permute-start(bf16[128,256]{1,0:T(8,128)(2,1)S(1)} %get-tuple-element.5), channel_id=1, source_target_pairs={{0,2},{2,4},{4,6},{6,0},{1,3},{3,5},{5,7},{7,1},{8,10},{10,12},{12... | collective-permute-start | bytes 196616 | tf_op jit(solution)/shard_map/ppermute | solution.py:22
  159.4 10.4 %collective-permute-start.11 = (bf16[128,256]{1,0:T(8,128)(2,1)S(1)}, bf16[128,256]{1,0:T(8,128)(2,1)S(1)}, u32[]{:S(2)}, u32[]{:S(2)}) collective-permute-start(bf16[128,256]{1,0:T(8,128)(2,1)S(1)} %get-tuple-element.7), channel_id=1, source_target_pairs={{0,4},{2,6},{4,0},{6,2},{1,5},{3,7},{5,1},{7,3},{8,12},{10,14},{12... | collective-permute-start | bytes 196616 | tf_op jit(solution)/shard_map/ppermute | solution.py:22
  164.6 8.9 %collective-permute-start.12 = (bf16[128,256]{1,0:T(8,128)(2,1)S(1)}, bf16[128,256]{1,0:T(8,128)(2,1)S(1)}, u32[]{:S(2)}, u32[]{:S(2)}) collective-permute-start(bf16[128,256]{1,0:T(8,128)(2,1)S(1)} %get-tuple-element.6), channel_id=1, source_target_pairs={{0,6},{2,0},{4,2},{6,4},{1,7},{3,1},{5,3},{7,5},{8,14},{10,8},{12,... | collective-permute-start | bytes 196616 | tf_op jit(solution)/shard_map/ppermute | solution.py:22

commit v3 on v2

v3 whole, which is shorter than its diff:
```python
import jax
import jax.numpy as jnp
from jax import lax
from jax.sharding import Mesh, PartitionSpec as P

BF16 = jnp.bfloat16
F32 = jnp.float32
DP = ("x", "zl", "y")
MP = ("zh", "core")


def exchange(pieces, axes):
    return lax.all_to_all(pieces, axes, 0, 0, tiled=True)


def dot(left, right, contract):
    return lax.dot_general(left, right, (contract, ((), ())), preferred_element_type=F32)


def shifted(block, axis, step):
    size = lax.axis_size(axis)
    return lax.ppermute(block, axis, [(i, (i + step) % size) for i in range(size)])


def per_device(query_states, passage_states, proj_weight, positive_index, logit_scale, logit_bias):
    nx, nzl, ny, nzh = (lax.axis_size(a) for a in ("x", "zl", "y", "zh"))
    rows = query_states.shape[0]
    depth, cols = proj_weight.shape
    blocks = nzl * ny
    sub = rows // nzh
    scale_value = logit_scale[0]
    bias_value = logit_bias[0]

    w_part = exchange(jnp.broadcast_to(proj_weight[None], (blocks, depth, cols)), ("zl", "y"))
    w_part = w_part.reshape(1, blocks * depth, cols)
    w_all = exchange(jnp.broadcast_to(w_part, (nx, blocks * depth, cols)), "x")
    w_all = w_all.reshape(nx * blocks * depth, cols)
    passages = dot(passage_states, w_all, ((1,), (0,))).astype(BF16)
    queries = dot(query_states, w_all, ((1,), (0,))).astype(BF16)

    q_send = jnp.broadcast_to(queries[None], (nzh, rows, cols))
    own = jnp.concatenate([q_send, passages.reshape(nzh, sub, cols)], axis=1)
    own = exchange(own, "zh").transpose(1, 0, 2).reshape(rows + sub, nzh * cols)
    q_own, p_own = own[:rows], own[rows:]

    p_tile = exchange(jnp.broadcast_to(p_own[None], (blocks, sub, nzh * cols)), ("zl", "y"))
    p_tile = p_tile.reshape(blocks * sub, nzh * cols)
    q_tile = jnp.concatenate([q_own] + [shifted(q_own, "x", k) for k in range(1, nx)], axis=0)

    part = dot(q_tile, p_tile, ((1,), (1,))).astype(BF16)
    other = lax.ppermute(part, "core", [(0, 1), (1, 0)])
    scores = part.astype(F32) + other.astype(F32)

    own_block = lax.axis_index("zl") * ny + lax.axis_index("y")
    place = positive_index - lax.axis_index("zh") * sub
    target = jnp.where((place >= 0) & (place < sub), own_block * sub + place, -1)
    target = jnp.pad(target, (0, (nx - 1) * rows), constant_values=-1)[:, None]
    labels = (jnp.arange(blocks * sub, dtype=jnp.int32)[None, :] == target).astype(F32)
    logits = scale_value * scores + bias_value
    weight = (jax.nn.sigmoid(logits) - labels).astype(BF16)

    gp = dot(weight, q_tile, ((0,), (0,))).astype(BF16)
    gp = exchange(gp.reshape(blocks, sub, nzh * cols), ("zl", "y"))
    gp = jnp.sum(gp.astype(F32), axis=0)

    gq = dot(weight, p_tile, ((1,), (0,)))
    gq = gq[:rows] + sum(
        shifted(gq[k * rows : (k + 1) * rows].astype(BF16), "x", -k).astype(F32)
        for k in range(1, nx)
    )

    both = jnp.concatenate([gq, gp], axis=0).astype(BF16).reshape(rows + sub, nzh, cols)
    both = exchange(both.transpose(1, 0, 2), "zh").astype(F32)
    grad_q = jnp.sum(both[:, :rows], axis=0)
    grad_p = both[:, rows:].reshape(rows, cols)
    return (scale_value * grad_q, scale_value * grad_p)


def solution(mesh):
    fine = Mesh(mesh.devices.reshape(4, 2, 8, 4, 2), DP + MP)
    in_specs = (P(DP, None), P(DP, None), P(DP, MP), P(DP), P(), P())
    out_specs = (P(DP, MP), P(DP, MP))
    return jax.shard_map(
        per_device, mesh=fine, in_specs=in_specs, out_specs=out_specs, check_vma=False
    )
```

time: 176 us -> 145 us (0.82)
  the two profiles are of different devices: /device:TPU:1 before, /device:TPU:8 now
where the time goes in v3:
time: 145 us; the launch traced here: 144 us
  blocking collectives  71.8 us (50%)
  waiting for transfers between devices  31.1 us (21%)
  starting transfers between devices  28.5 us (20%)
  matrix products  6.59 us (5%)
  local copies, waits for them, and re-layouts  2.51 us (2%)
  between operations  2.18 us (2%)
  other arithmetic  1.8 us (1%)
    all_to_all x4, blocking collectives, exchange(): return lax.all_to_all(pieces, axes, 0, 0, tiled=True)  71.8 us
    ppermute x6, waiting for transfers between devices, shifted(): lax.ppermute(block, axis, [(i, (i + step) % size) for i in range(size)])  18.7 us
    ppermute x6, starting transfers between devices, shifted(): lax.ppermute(block, axis, [(i, (i + step) % size) for i in range(size)])  16.9 us
    all_to_all x2, waiting for transfers between devices, exchange(): return lax.all_to_all(pieces, axes, 0, 0, tiled=True)  11.7 us
    all_to_all x2, starting transfers between devices, exchange(): return lax.all_to_all(pieces, axes, 0, 0, tiled=True)  9.68 us
    dot_general x5, matrix products, dot(): lax.dot_general(left, right, (contract, ((), ())), preferred_element_type...  6.59 us
  transfers between devices with their start and end apart: 9, of which 8 were waited for; matrix products, arithmetic and copies ran while one was open for 2% of the time, Pallas kernels for 0%

profile of v3, /device:TPU:8, one launch (start us, length us, event | category | flops | bytes accessed | tf_op | source)
XLA Modules:
  0.0 144.4 jit_solution(17041252238234231442)
XLA Ops:
  0.6 0.8 broadcast_in_dim.15
  1.4 19.2 %all_to_all.30 = bf16[16,32,256]{2,1,0:T(8,128)(2,1)S(1)} all-to-all(bf16[16,32,256]{2,1,0:T(8,128)(2,1)S(1)} %broadcast_in_dim.15), channel_id=1, replica_groups=mesh['x'=4,'zl'=2,'y'=8,'zh'=4,'core'=2] {'zl','y'}, dimensions={0} | all-to-all | bytes 524288 | tf_op jit(solution)/shard_map/all_to_all | solution.py:13
  20.8 18.3 %all_to_all.31 = bf16[4,512,256]{2,1,0:T(8,128)(2,1)S(1)} all-to-all(bf16[4,512,256]{2,1,0:T(8,128)(2,1)S(1)} %broadcast_in_dim.18), channel_id=1, replica_groups=mesh['x'=4,'zl'=2,'y'=8,'zh'=4,'core'=2] {'x'}, dimensions={0} | all-to-all | bytes 2097152 | tf_op jit(solution)/shard_map/all_to_all | solution.py:13
  39.8 20.0 %all_to_all.32 = bf16[4,160,256]{2,1,0:T(8,128)(2,1)S(1)} all-to-all(bf16[4,160,256]{2,1,0:T(8,128)(2,1)S(1)} %pad_maximum_fusion.1), channel_id=1, replica_groups=mesh['x'=4,'zl'=2,'y'=8,'zh'=4,'core'=2] {'zh'}, dimensions={0} | all-to-all | bytes 655360 | tf_op jit(solution)/shard_map/all_to_all | solution.py:13
  60.2 1.1 broadcast_in_dim.38
  61.3 4.6 %all-to-all-start.3 = ((bf16[16,32,1024]{2,1,0:T(8,128)(2,1)}), bf16[16,32,1024]{2,1,0:T(8,128)(2,1)S(1)}, u32[]{:S(2)}, u32[]{:S(2)}) async-start(bf16[16,32,1024]{2,1,0:T(8,128)(2,1)} %broadcast_in_dim.38), calls=%async_computation.3 | async-start | bytes 2097152 | tf_op jit(solution)/shard_map/all_to_all | solution.py:13
  65.9 3.1 %collective-permute-start.2 = (bf16[128,1024]{0,1:T(8,128)(2,1)S(1)}, bf16[128,1024]{0,1:T(8,128)(2,1)S(1)}, u32[]{:S(2)}, u32[]{:S(2)}) collective-permute-start(bf16[128,1024]{0,1:T(8,128)(2,1)S(1)} %bitcast.47), channel_id=1, source_target_pairs={{0,384},{128,0},{256,128},{384,256},{1,385},{129,1},{257,129},{385... | collective-permute-start | bytes 786440 | tf_op jit(solution)/shard_map/ppermute | solution.py:22
  69.0 3.3 %collective-permute-start.1 = (bf16[128,1024]{0,1:T(8,128)(2,1)S(1)}, bf16[128,1024]{0,1:T(8,128)(2,1)S(1)}, u32[]{:S(2)}, u32[]{:S(2)}) collective-permute-start(bf16[128,1024]{0,1:T(8,128)(2,1)S(1)} %bitcast.48), channel_id=1, source_target_pairs={{0,256},{128,384},{256,0},{384,128},{1,257},{129,385},{257,1},{385... | collective-permute-start | bytes 786440 | tf_op jit(solution)/shard_map/ppermute | solution.py:22
  72.3 1.9 %collective-permute-start = (bf16[128,1024]{0,1:T(8,128)(2,1)S(1)}, bf16[128,1024]{0,1:T(8,128)(2,1)S(1)}, u32[]{:S(2)}, u32[]{:S(2)}) collective-permute-start(bf16[128,1024]{0,1:T(8,128)(2,1)S(1)} %bitcast.49), channel_id=1, source_target_pairs={{0,128},{128,256},{256,384},{384,0},{1,129},{129,257},{257,385},{3... | collective-permute-start | bytes 786440 | tf_op jit(solution)/shard_map/ppermute | solution.py:22
  74.8 4.6 %collective-permute-done.1 = bf16[128,1024]{0,1:T(8,128)(2,1)S(1)} collective-permute-done((bf16[128,1024]{0,1:T(8,128)(2,1)S(1)}, bf16[128,1024]{0,1:T(8,128)(2,1)S(1)}, u32[]{:S(2)}, u32[]{:S(2)}) %collective-permute-start.1) | collective-permute-done | bytes 262176 | tf_op jit(solution)/shard_map/ppermute | solution.py:22
  79.5 2.8 %collective-permute-done = bf16[128,1024]{0,1:T(8,128)(2,1)S(1)} collective-permute-done((bf16[128,1024]{0,1:T(8,128)(2,1)S(1)}, bf16[128,1024]{0,1:T(8,128)(2,1)S(1)}, u32[]{:S(2)}, u32[]{:S(2)}) %collective-permute-start) | collective-permute-done | bytes 262176 | tf_op jit(solution)/shard_map/ppermute | solution.py:22
  82.2 6.7 %all-to-all-done.3 = bf16[16,32,1024]{2,1,0:T(8,128)(2,1)S(1)} async-done(((bf16[16,32,1024]{2,1,0:T(8,128)(2,1)}), bf16[16,32,1024]{2,1,0:T(8,128)(2,1)S(1)}, u32[]{:S(2)}, u32[]{:S(2)}) %all-to-all-start.3) | async-done | bytes 1048608 | tf_op jit(solution)/shard_map/all_to_all | solution.py:13
  89.0 0.8 convolution_convert_fusion.1
  89.7 1.9 %collective-permute-start.3 = (bf16[512,512]{1,0:T(8,128)(2,1)S(1)}, bf16[512,512]{1,0:T(8,128)(2,1)}, u32[]{:S(2)}, u32[]{:S(2)}) collective-permute-start(bf16[512,512]{1,0:T(8,128)(2,1)S(1)} %convolution_convert_fusion.1), channel_id=1, source_target_pairs={{0,1},{1,0},{2,3},{3,2},{4,5},{5,4},{6,7},{7,6},{8,9},{9,8},{10,11... | collective-permute-start | bytes 1572872 | tf_op jit(solution)/shard_map/ppermute | solution.py:51
  93.7 3.2 %convolution_convert_fusion = bf16[512,1024]{1,0:T(8,128)(2,1)} fusion(bf16[128,1024]{0,1:T(8,128)(2,1)S(1)} %collective-permute-done.2, bf16[128,1024]{0,1:T(8,128)(2,1)S(1)} %collective-permute-done.1, bf16[128,1024]{0,1:T(8,128)(2,1)} %copy-done.3, bf16[128,1024]{0,1:T(8,128)(2,1)S(1)} %bitcast.51, bf16[512,512]{1,0:T(8,128)(2,1)} %collective-permute-done.3, ...), kind=kOutput, calls=%fused_computation | convolution fusion | flops 544735232 | bytes 3147784 | tf_op jit(solution)/shard_map/dot_general | solution.py:17
  96.9 5.1 %all-to-all-start.4 = ((bf16[16,32,1024]{2,1,0:T(8,128)(2,1)}), bf16[16,32,1024]{2,1,0:T(8,128)(2,1)S(1)}, u32[]{:S(2)}, u32[]{:S(2)}) async-start(bf16[16,32,1024]{2,1,0:T(8,128)(2,1)} %bitcast.41), calls=%async_computation.4 | async-start | bytes 2097152 | tf_op jit(solution)/shard_map/all_to_all | solution.py:13
  102.0 2.0 %fusion.5 = (bf16[512,1024]{1,0:T(8,128)(2,1)S(1)}, f32[512,1024]{1,0:T(8,128)S(1)}) fusion(bf16[512,1024]{1,0:T(8,128)(2,1)S(1)} %bitcast.40, bf16[512,512]{1,0:T(8,128)(2,1)} %collective-permute-done.3, bf16[512,512]{1,0:T(8,128)(2,1)S(1)} %convolution_convert_fusion.1, s32[512]{0:T(512)S(1)} %pad.4, f32[]{:T(128)} %bitcast.31, f32[]{:T(128)} %bitcast.28), kind=kOutput, calls=%fused_computation.21 | convolution fusion | flops 540540928 | bytes 5244936 | tf_op jit(solution)/shard_map/dot_general | solution.py:17
  104.1 3.1 %collective-permute-start.4 = (bf16[128,1024]{1,0:T(8,128)(2,1)S(1)}, bf16[128,1024]{1,0:T(8,128)(2,1)S(1)}, u32[]{:S(2)}, u32[]{:S(2)}) collective-permute-start(bf16[128,1024]{1,0:T(8,128)(2,1)S(1)} %get-tuple-element.2), channel_id=1, source_target_pairs={{0,384},{128,0},{256,128},{384,256},{1,385},{129,1},{257,129},{385... | collective-permute-start | bytes 786440 | tf_op jit(solution)/shard_map/ppermute | solution.py:22
  107.2 2.8 %collective-permute-start.6 = (bf16[128,1024]{1,0:T(8,128)(2,1)S(1)}, bf16[128,1024]{1,0:T(8,128)(2,1)S(1)}, u32[]{:S(2)}, u32[]{:S(2)}) collective-permute-start(bf16[128,1024]{1,0:T(8,128)(2,1)S(1)} %get-tuple-element.3), channel_id=1, source_target_pairs={{0,128},{128,256},{256,384},{384,0},{1,129},{129,257},{257,385},{3... | collective-permute-start | bytes 786440 | tf_op jit(solution)/shard_map/ppermute | solution.py:22
  109.9 2.7 %collective-permute-start.5 = (bf16[128,1024]{1,0:T(8,128)(2,1)S(1)}, bf16[128,1024]{1,0:T(8,128)(2,1)S(1)}, u32[]{:S(2)}, u32[]{:S(2)}) collective-permute-start(bf16[128,1024]{1,0:T(8,128)(2,1)S(1)} %get-tuple-element.4), channel_id=1, source_target_pairs={{0,256},{128,384},{256,0},{384,128},{1,257},{129,385},{257,1},{385... | collective-permute-start | bytes 786440 | tf_op jit(solution)/shard_map/ppermute | solution.py:22
  112.7 1.1 collective-permute-done.4
  113.8 9.6 %collective-permute-done.6 = bf16[128,1024]{1,0:T(8,128)(2,1)S(1)} collective-permute-done((bf16[128,1024]{1,0:T(8,128)(2,1)S(1)}, bf16[128,1024]{1,0:T(8,128)(2,1)S(1)}, u32[]{:S(2)}, u32[]{:S(2)}) %collective-permute-start.6) | collective-permute-done | bytes 262176 | tf_op jit(solution)/shard_map/ppermute | solution.py:22
  123.6 5.0 %all-to-all-done.4 = bf16[16,32,1024]{2,1,0:T(8,128)(2,1)S(1)} async-done(((bf16[16,32,1024]{2,1,0:T(8,128)(2,1)}), bf16[16,32,1024]{2,1,0:T(8,128)(2,1)S(1)}, u32[]{:S(2)}, u32[]{:S(2)}) %all-to-all-start.4) | async-done | bytes 1048608 | tf_op jit(solution)/shard_map/all_to_all | solution.py:13
  128.8 14.2 %all_to_all.33 = bf16[4,160,256]{2,1,0:T(8,128)(2,1)S(1)} all-to-all(bf16[4,160,256]{2,1,0:T(8,128)(2,1)S(1)} %maximum_bitcast_fusion), channel_id=1, replica_groups=mesh['x'=4,'zl'=2,'y'=8,'zh'=4,'core'=2] {'zh'}, dimensions={0} | all-to-all | bytes 655360 | tf_op jit(solution)/shard_map/all_to_all | solution.py:13
  (32 shorter events, 4.3 us)
Async XLA Ops:
  0.6 38.4 %copy-start = (bf16[128,2048]{1,0:T(8,128)(2,1)S(1)}, bf16[128,2048]{1,0:T(8,128)(2,1)}, u32[]{:S(2)}) copy-start(bf16[128,2048]{1,0:T(8,128)(2,1)} %param.7) | copy-start | bytes 1572868
  20.7 18.6 %copy-start.1 = (bf16[128,2048]{1,0:T(8,128)(2,1)S(1)}, bf16[128,2048]{1,0:T(8,128)(2,1)}, u32[]{:S(2)}) copy-start(bf16[128,2048]{1,0:T(8,128)(2,1)} %param.6) | copy-start | bytes 1572868
  61.3 27.7 %all-to-all-start.3 = ((bf16[16,32,1024]{2,1,0:T(8,128)(2,1)}), bf16[16,32,1024]{2,1,0:T(8,128)(2,1)S(1)}, u32[]{:S(2)}, u32[]{:S(2)}) async-start(bf16[16,32,1024]{2,1,0:T(8,128)(2,1)} %broadcast_in_dim.38), calls=%async_computation.3 | async-start | bytes 2097152 | tf_op jit(solution)/shard_map/all_to_all | solution.py:13
  65.9 8.9 %collective-permute-start.2 = (bf16[128,1024]{0,1:T(8,128)(2,1)S(1)}, bf16[128,1024]{0,1:T(8,128)(2,1)S(1)}, u32[]{:S(2)}, u32[]{:S(2)}) collective-permute-start(bf16[128,1024]{0,1:T(8,128)(2,1)S(1)} %bitcast.47), channel_id=1, source_target_pairs={{0,384},{128,0},{256,128},{384,256},{1,385},{129,1},{257,129},{385... | collective-permute-start | bytes 786440 | tf_op jit(solution)/shard_map/ppermute | solution.py:22
  69.0 10.5 %collective-permute-start.1 = (bf16[128,1024]{0,1:T(8,128)(2,1)S(1)}, bf16[128,1024]{0,1:T(8,128)(2,1)S(1)}, u32[]{:S(2)}, u32[]{:S(2)}) collective-permute-start(bf16[128,1024]{0,1:T(8,128)(2,1)S(1)} %bitcast.48), channel_id=1, source_target_pairs={{0,256},{128,384},{256,0},{384,128},{1,257},{129,385},{257,1},{385... | collective-permute-start | bytes 786440 | tf_op jit(solution)/shard_map/ppermute | solution.py:22
  72.3 9.9 %collective-permute-start = (bf16[128,1024]{0,1:T(8,128)(2,1)S(1)}, bf16[128,1024]{0,1:T(8,128)(2,1)S(1)}, u32[]{:S(2)}, u32[]{:S(2)}) collective-permute-start(bf16[128,1024]{0,1:T(8,128)(2,1)S(1)} %bitcast.49), channel_id=1, source_target_pairs={{0,128},{128,256},{256,384},{384,0},{1,129},{129,257},{257,385},{3... | collective-permute-start | bytes 786440 | tf_op jit(solution)/shard_map/ppermute | solution.py:22
  82.2 10.1 %copy-start.3 = (bf16[128,1024]{0,1:T(8,128)(2,1)}, bf16[128,1024]{0,1:T(8,128)(2,1)S(1)}, u32[]{:S(2)}) copy-start(bf16[128,1024]{0,1:T(8,128)(2,1)S(1)} %collective-permute-done) | copy-start | bytes 786436
  89.0 4.0 %copy-start.2 = (s32[128]{0:T(128)S(1)}, s32[128]{0:T(128)}, u32[]{:S(2)}) copy-start(s32[128]{0:T(128)} %param.9) | copy-start | bytes 1540
  89.7 3.9 %collective-permute-start.3 = (bf16[512,512]{1,0:T(8,128)(2,1)S(1)}, bf16[512,512]{1,0:T(8,128)(2,1)}, u32[]{:S(2)}, u32[]{:S(2)}) collective-permute-start(bf16[512,512]{1,0:T(8,128)(2,1)S(1)} %convolution_convert_fusion.1), channel_id=1, source_target_pairs={{0,1},{1,0},{2,3},{3,2},{4,5},{5,4},{6,7},{7,6},{8,9},{9,8},{10,11... | collective-permute-start | bytes 1572872 | tf_op jit(solution)/shard_map/ppermute | solution.py:51
  96.9 31.7 %all-to-all-start.4 = ((bf16[16,32,1024]{2,1,0:T(8,128)(2,1)}), bf16[16,32,1024]{2,1,0:T(8,128)(2,1)S(1)}, u32[]{:S(2)}, u32[]{:S(2)}) async-start(bf16[16,32,1024]{2,1,0:T(8,128)(2,1)} %bitcast.41), calls=%async_computation.4 | async-start | bytes 2097152 | tf_op jit(solution)/shard_map/all_to_all | solution.py:13
  104.1 9.7 %collective-permute-start.4 = (bf16[128,1024]{1,0:T(8,128)(2,1)S(1)}, bf16[128,1024]{1,0:T(8,128)(2,1)S(1)}, u32[]{:S(2)}, u32[]{:S(2)}) collective-permute-start(bf16[128,1024]{1,0:T(8,128)(2,1)S(1)} %get-tuple-element.2), channel_id=1, source_target_pairs={{0,384},{128,0},{256,128},{384,256},{1,385},{129,1},{257,129},{385... | collective-permute-start | bytes 786440 | tf_op jit(solution)/shard_map/ppermute | solution.py:22
  107.2 16.2 %collective-permute-start.6 = (bf16[128,1024]{1,0:T(8,128)(2,1)S(1)}, bf16[128,1024]{1,0:T(8,128)(2,1)S(1)}, u32[]{:S(2)}, u32[]{:S(2)}) collective-permute-start(bf16[128,1024]{1,0:T(8,128)(2,1)S(1)} %get-tuple-element.3), channel_id=1, source_target_pairs={{0,128},{128,256},{256,384},{384,0},{1,129},{129,257},{257,385},{3... | collective-permute-start | bytes 786440 | tf_op jit(solution)/shard_map/ppermute | solution.py:22
  109.9 13.5 %collective-permute-start.5 = (bf16[128,1024]{1,0:T(8,128)(2,1)S(1)}, bf16[128,1024]{1,0:T(8,128)(2,1)S(1)}, u32[]{:S(2)}, u32[]{:S(2)}) collective-permute-start(bf16[128,1024]{1,0:T(8,128)(2,1)S(1)} %get-tuple-element.4), channel_id=1, source_target_pairs={{0,256},{128,384},{256,0},{384,128},{1,257},{129,385},{257,1},{385... | collective-permute-start | bytes 786440 | tf_op jit(solution)/shard_map/ppermute | solution.py:22

commit v4 on v3

--- a/solution.py
+++ b/solution.py
@@ -31,9 +31,9 @@
     scale_value = logit_scale[0]
     bias_value = logit_bias[0]
 
-    w_part = exchange(jnp.broadcast_to(proj_weight[None], (blocks, depth, cols)), ("zl", "y"))
-    w_part = w_part.reshape(1, blocks * depth, cols)
-    w_all = exchange(jnp.broadcast_to(w_part, (nx, blocks * depth, cols)), "x")
+    w_part = exchange(jnp.broadcast_to(proj_weight[None], (ny, depth, cols)), "y")
+    w_part = w_part.reshape(1, ny * depth, cols)
+    w_all = exchange(jnp.broadcast_to(w_part, (nx * nzl, ny * depth, cols)), ("x", "zl"))
     w_all = w_all.reshape(nx * blocks * depth, cols)
     passages = dot(passage_states, w_all, ((1,), (0,))).astype(BF16)
     queries = dot(query_states, w_all, ((1,), (0,))).astype(BF16)
@@ -46,6 +46,7 @@
     p_tile = exchange(jnp.broadcast_to(p_own[None], (blocks, sub, nzh * cols)), ("zl", "y"))
     p_tile = p_tile.reshape(blocks * sub, nzh * cols)
     q_tile = jnp.concatenate([q_own] + [shifted(q_own, "x", k) for k in range(1, nx)], axis=0)
+    q_tile = lax.optimization_barrier(q_tile)
 
     part = dot(q_tile, p_tile, ((1,), (1,))).astype(BF16)
     other = lax.ppermute(part, "core", [(0, 1), (1, 0)])
@@ -57,7 +58,7 @@
     target = jnp.pad(target, (0, (nx - 1) * rows), constant_values=-1)[:, None]
     labels = (jnp.arange(blocks * sub, dtype=jnp.int32)[None, :] == target).astype(F32)
     logits = scale_value * scores + bias_value
-    weight = (jax.nn.sigmoid(logits) - labels).astype(BF16)
+    weight = lax.optimization_barrier((jax.nn.sigmoid(logits) - labels).astype(BF16))
 
     gp = dot(weight, q_tile, ((0,), (0,))).astype(BF16)
     gp = exchange(gp.reshape(blocks, sub, nzh * cols), ("zl", "y"))

time: 145 us -> 142 us (0.979)
  the two profiles are of different devices: /device:TPU:8 before, /device:TPU:16 now
where the time goes in v4:
time: 142 us; the launch traced here: 141 us
  blocking collectives  69.1 us (49%)
  starting transfers between devices  31.6 us (22%)
  waiting for transfers between devices  28.5 us (20%)
  matrix products  3.82 us (3%)
  other arithmetic  3.57 us (3%)
  local copies, waits for them, and re-layouts  2.5 us (2%)
  between operations  2.19 us (2%)
    all_to_all x4, blocking collectives, exchange(): return lax.all_to_all(pieces, axes, 0, 0, tiled=True)  69.1 us
    ppermute x6, waiting for transfers between devices, shifted(): lax.ppermute(block, axis, [(i, (i + step) % size) for i in range(size)])  18.3 us
    ppermute x6, starting transfers between devices, shifted(): lax.ppermute(block, axis, [(i, (i + step) % size) for i in range(size)])  17 us
    all_to_all x2, starting transfers between devices, exchange(): return lax.all_to_all(pieces, axes, 0, 0, tiled=True)  12.7 us
    all_to_all x2, waiting for transfers between devices, exchange(): return lax.all_to_all(pieces, axes, 0, 0, tiled=True)  9.53 us
    dot_general x5, matrix products, dot(): lax.dot_general(left, right, (contract, ((), ())), preferred_element_type...  3.82 us
  transfers between devices with their start and end apart: 9, of which 8 were waited for; matrix products, arithmetic and copies ran while one was open for 1% of the time, Pallas kernels for 0%

profile of v4, /device:TPU:16, one launch (start us, length us, event | category | flops | bytes accessed | tf_op | source)
XLA Modules:
  0.0 141.3 jit_solution(7021125710154887265)
XLA Ops:
  0.6 0.8 broadcast_in_dim.15
  1.4 14.6 %all_to_all.30 = bf16[8,32,256]{2,1,0:T(8,128)(2,1)S(1)} all-to-all(bf16[8,32,256]{2,1,0:T(8,128)(2,1)S(1)} %broadcast_in_dim.15), channel_id=1, replica_groups=mesh['x'=4,'zl'=2,'y'=8,'zh'=4,'core'=2] {'y'}, dimensions={0} | all-to-all | bytes 262144 | tf_op jit(solution)/shard_map/all_to_all | solution.py:13
  16.2 19.3 %all_to_all.31 = bf16[8,256,256]{2,1,0:T(8,128)(2,1)S(1)} all-to-all(bf16[8,256,256]{2,1,0:T(8,128)(2,1)S(1)} %broadcast_in_dim.18), channel_id=1, replica_groups=mesh['x'=4,'zl'=2,'y'=8,'zh'=4,'core'=2] {'x','zl'}, dimensions={0} | all-to-all | bytes 2097152 | tf_op jit(solution)/shard_map/all_to_all | solution.py:13
  36.2 19.5 %all_to_all.32 = bf16[4,160,256]{2,1,0:T(8,128)(2,1)S(1)} all-to-all(bf16[4,160,256]{2,1,0:T(8,128)(2,1)S(1)} %pad_maximum_fusion.1), channel_id=1, replica_groups=mesh['x'=4,'zl'=2,'y'=8,'zh'=4,'core'=2] {'zh'}, dimensions={0} | all-to-all | bytes 655360 | tf_op jit(solution)/shard_map/all_to_all | solution.py:13
  56.0 1.1 broadcast_in_dim.38
  57.1 6.1 %all-to-all-start.3 = ((bf16[16,32,1024]{2,1,0:T(8,128)(2,1)}), bf16[16,32,1024]{2,1,0:T(8,128)(2,1)S(1)}, u32[]{:S(2)}, u32[]{:S(2)}) async-start(bf16[16,32,1024]{2,1,0:T(8,128)(2,1)} %broadcast_in_dim.38), calls=%async_computation.3 | async-start | bytes 2097152 | tf_op jit(solution)/shard_map/all_to_all | solution.py:13
  63.3 3.1 %collective-permute-start.2 = (bf16[128,1024]{0,1:T(8,128)(2,1)S(1)}, bf16[128,1024]{0,1:T(8,128)(2,1)S(1)}, u32[]{:S(2)}, u32[]{:S(2)}) collective-permute-start(bf16[128,1024]{0,1:T(8,128)(2,1)S(1)} %bitcast.45), channel_id=1, source_target_pairs={{0,384},{128,0},{256,128},{384,256},{1,385},{129,1},{257,129},{385... | collective-permute-start | bytes 786440 | tf_op jit(solution)/shard_map/ppermute | solution.py:22
  66.4 3.0 %collective-permute-start.1 = (bf16[128,1024]{0,1:T(8,128)(2,1)S(1)}, bf16[128,1024]{0,1:T(8,128)(2,1)S(1)}, u32[]{:S(2)}, u32[]{:S(2)}) collective-permute-start(bf16[128,1024]{0,1:T(8,128)(2,1)S(1)} %bitcast.46), channel_id=1, source_target_pairs={{0,256},{128,384},{256,0},{384,128},{1,257},{129,385},{257,1},{385... | collective-permute-start | bytes 786440 | tf_op jit(solution)/shard_map/ppermute | solution.py:22
  69.4 2.1 %collective-permute-start = (bf16[128,1024]{0,1:T(8,128)(2,1)S(1)}, bf16[128,1024]{0,1:T(8,128)(2,1)S(1)}, u32[]{:S(2)}, u32[]{:S(2)}) collective-permute-start(bf16[128,1024]{0,1:T(8,128)(2,1)S(1)} %bitcast.47), channel_id=1, source_target_pairs={{0,128},{128,256},{256,384},{384,0},{1,129},{129,257},{257,385},{3... | collective-permute-start | bytes 786440 | tf_op jit(solution)/shard_map/ppermute | solution.py:22
  71.9 4.6 %collective-permute-done.1 = bf16[128,1024]{0,1:T(8,128)(2,1)S(1)} collective-permute-done((bf16[128,1024]{0,1:T(8,128)(2,1)S(1)}, bf16[128,1024]{0,1:T(8,128)(2,1)S(1)}, u32[]{:S(2)}, u32[]{:S(2)}) %collective-permute-start.1) | collective-permute-done | bytes 262176 | tf_op jit(solution)/shard_map/ppermute | solution.py:22
  76.5 2.8 %collective-permute-done = bf16[128,1024]{0,1:T(8,128)(2,1)S(1)} collective-permute-done((bf16[128,1024]{0,1:T(8,128)(2,1)S(1)}, bf16[128,1024]{0,1:T(8,128)(2,1)S(1)}, u32[]{:S(2)}, u32[]{:S(2)}) %collective-permute-start) | collective-permute-done | bytes 262176 | tf_op jit(solution)/shard_map/ppermute | solution.py:22
  79.4 5.2 %all-to-all-done.3 = bf16[16,32,1024]{2,1,0:T(8,128)(2,1)S(1)} async-done(((bf16[16,32,1024]{2,1,0:T(8,128)(2,1)}), bf16[16,32,1024]{2,1,0:T(8,128)(2,1)S(1)}, u32[]{:S(2)}, u32[]{:S(2)}) %all-to-all-start.3) | async-done | bytes 1048608 | tf_op jit(solution)/shard_map/all_to_all | solution.py:13
  84.6 0.8 convolution_convert_fusion.1
  85.3 1.9 %collective-permute-start.3 = (bf16[512,512]{1,0:T(8,128)(2,1)S(1)}, bf16[512,512]{1,0:T(8,128)(2,1)}, u32[]{:S(2)}, u32[]{:S(2)}) collective-permute-start(bf16[512,512]{1,0:T(8,128)(2,1)S(1)} %convolution_convert_fusion.1), channel_id=1, source_target_pairs={{0,1},{1,0},{2,3},{3,2},{4,5},{5,4},{6,7},{7,6},{8,9},{9,8},{10,11... | collective-permute-start | bytes 1572872 | tf_op jit(solution)/shard_map/ppermute | solution.py:52
  89.3 1.7 %subtract_convert_fusion = bf16[512,512]{1,0:T(8,128)(2,1)S(1)} fusion(bf16[512,512]{1,0:T(8,128)(2,1)} %collective-permute-done.3, bf16[512,512]{1,0:T(8,128)(2,1)} %copy-done.2, s32[512]{0:T(512)S(1)} %pad.4, f32[]{:T(128)} %bitcast.34, f32[]{:T(128)} %bitcast.32), kind=kLoop, calls=%fused_computation.5 | loop fusion | flops 3145728 | bytes 1574920 | tf_op jit(solution)/shard_map/convert_element_type | solution.py:61
  90.9 1.7 %convolution_convert_fusion = bf16[512,1024]{1,0:T(8,128)(2,1)} fusion(bf16[512,512]{1,0:T(8,128)(2,1)S(1)} %subtract_convert_fusion, bf16[512,1024]{0,1:T(8,128)(2,1)S(1)} %pad_maximum_fusion), kind=kOutput, calls=%fused_computation | convolution fusion | flops 537395200 | bytes 2621440 | tf_op jit(solution)/shard_map/dot_general | solution.py:17
  92.7 6.5 %all-to-all-start.4 = ((bf16[16,32,1024]{2,1,0:T(8,128)(2,1)}), bf16[16,32,1024]{2,1,0:T(8,128)(2,1)S(1)}, u32[]{:S(2)}, u32[]{:S(2)}) async-start(bf16[16,32,1024]{2,1,0:T(8,128)(2,1)} %bitcast.42), calls=%async_computation.4 | async-start | bytes 2097152 | tf_op jit(solution)/shard_map/all_to_all | solution.py:13
  100.0 3.1 %collective-permute-start.4 = (bf16[128,1024]{1,0:T(8,128)(2,1)S(1)}, bf16[128,1024]{1,0:T(8,128)(2,1)S(1)}, u32[]{:S(2)}, u32[]{:S(2)}) collective-permute-start(bf16[128,1024]{1,0:T(8,128)(2,1)S(1)} %get-tuple-element.2), channel_id=1, source_target_pairs={{0,384},{128,0},{256,128},{384,256},{1,385},{129,1},{257,129},{385... | collective-permute-start | bytes 786440 | tf_op jit(solution)/shard_map/ppermute | solution.py:22
  103.1 2.8 %collective-permute-start.6 = (bf16[128,1024]{1,0:T(8,128)(2,1)S(1)}, bf16[128,1024]{1,0:T(8,128)(2,1)S(1)}, u32[]{:S(2)}, u32[]{:S(2)}) collective-permute-start(bf16[128,1024]{1,0:T(8,128)(2,1)S(1)} %get-tuple-element.3), channel_id=1, source_target_pairs={{0,128},{128,256},{256,384},{384,0},{1,129},{129,257},{257,385},{3... | collective-permute-start | bytes 786440 | tf_op jit(solution)/shard_map/ppermute | solution.py:22
  105.9 3.0 %collective-permute-start.5 = (bf16[128,1024]{1,0:T(8,128)(2,1)S(1)}, bf16[128,1024]{1,0:T(8,128)(2,1)S(1)}, u32[]{:S(2)}, u32[]{:S(2)}) collective-permute-start(bf16[128,1024]{1,0:T(8,128)(2,1)S(1)} %get-tuple-element.4), channel_id=1, source_target_pairs={{0,256},{128,384},{256,0},{384,128},{1,257},{129,385},{257,1},{385... | collective-permute-start | bytes 786440 | tf_op jit(solution)/shard_map/ppermute | solution.py:22
  108.9 0.8 collective-permute-done.4
  109.7 9.7 %collective-permute-done.6 = bf16[128,1024]{1,0:T(8,128)(2,1)S(1)} collective-permute-done((bf16[128,1024]{1,0:T(8,128)(2,1)S(1)}, bf16[128,1024]{1,0:T(8,128)(2,1)S(1)}, u32[]{:S(2)}, u32[]{:S(2)}) %collective-permute-start.6) | collective-permute-done | bytes 262176 | tf_op jit(solution)/shard_map/ppermute | solution.py:22
  119.5 4.4 %all-to-all-done.4 = bf16[16,32,1024]{2,1,0:T(8,128)(2,1)S(1)} async-done(((bf16[16,32,1024]{2,1,0:T(8,128)(2,1)}), bf16[16,32,1024]{2,1,0:T(8,128)(2,1)S(1)}, u32[]{:S(2)}, u32[]{:S(2)}) %all-to-all-start.4) | async-done | bytes 1048608 | tf_op jit(solution)/shard_map/all_to_all | solution.py:13
  124.1 15.7 %all_to_all.33 = bf16[4,160,256]{2,1,0:T(8,128)(2,1)S(1)} all-to-all(bf16[4,160,256]{2,1,0:T(8,128)(2,1)S(1)} %maximum_bitcast_fusion), channel_id=1, replica_groups=mesh['x'=4,'zl'=2,'y'=8,'zh'=4,'core'=2] {'zh'}, dimensions={0} | all-to-all | bytes 655360 | tf_op jit(solution)/shard_map/all_to_all | solution.py:13
  (34 shorter events, 4.9 us)
Async XLA Ops:
  0.6 34.8 %copy-start = (bf16[128,2048]{1,0:T(8,128)(2,1)S(1)}, bf16[128,2048]{1,0:T(8,128)(2,1)}, u32[]{:S(2)}) copy-start(bf16[128,2048]{1,0:T(8,128)(2,1)} %param.7) | copy-start | bytes 1572868
  16.1 19.6 %copy-start.1 = (bf16[128,2048]{1,0:T(8,128)(2,1)S(1)}, bf16[128,2048]{1,0:T(8,128)(2,1)}, u32[]{:S(2)}) copy-start(bf16[128,2048]{1,0:T(8,128)(2,1)} %param.6) | copy-start | bytes 1572868
  57.1 27.4 %all-to-all-start.3 = ((bf16[16,32,1024]{2,1,0:T(8,128)(2,1)}), bf16[16,32,1024]{2,1,0:T(8,128)(2,1)S(1)}, u32[]{:S(2)}, u32[]{:S(2)}) async-start(bf16[16,32,1024]{2,1,0:T(8,128)(2,1)} %broadcast_in_dim.38), calls=%async_computation.3 | async-start | bytes 2097152 | tf_op jit(solution)/shard_map/all_to_all | solution.py:13
  63.3 8.6 %collective-permute-start.2 = (bf16[128,1024]{0,1:T(8,128)(2,1)S(1)}, bf16[128,1024]{0,1:T(8,128)(2,1)S(1)}, u32[]{:S(2)}, u32[]{:S(2)}) collective-permute-start(bf16[128,1024]{0,1:T(8,128)(2,1)S(1)} %bitcast.45), channel_id=1, source_target_pairs={{0,384},{128,0},{256,128},{384,256},{1,385},{129,1},{257,129},{385... | collective-permute-start | bytes 786440 | tf_op jit(solution)/shard_map/ppermute | solution.py:22
  66.4 10.1 %collective-permute-start.1 = (bf16[128,1024]{0,1:T(8,128)(2,1)S(1)}, bf16[128,1024]{0,1:T(8,128)(2,1)S(1)}, u32[]{:S(2)}, u32[]{:S(2)}) collective-permute-start(bf16[128,1024]{0,1:T(8,128)(2,1)S(1)} %bitcast.46), channel_id=1, source_target_pairs={{0,256},{128,384},{256,0},{384,128},{1,257},{129,385},{257,1},{385... | collective-permute-start | bytes 786440 | tf_op jit(solution)/shard_map/ppermute | solution.py:22
  69.4 9.9 %collective-permute-start = (bf16[128,1024]{0,1:T(8,128)(2,1)S(1)}, bf16[128,1024]{0,1:T(8,128)(2,1)S(1)}, u32[]{:S(2)}, u32[]{:S(2)}) collective-permute-start(bf16[128,1024]{0,1:T(8,128)(2,1)S(1)} %bitcast.47), channel_id=1, source_target_pairs={{0,128},{128,256},{256,384},{384,0},{1,129},{129,257},{257,385},{3... | collective-permute-start | bytes 786440 | tf_op jit(solution)/shard_map/ppermute | solution.py:22
  79.4 9.2 %copy-start.3 = (s32[128]{0:T(128)S(1)}, s32[128]{0:T(128)}, u32[]{:S(2)}) copy-start(s32[128]{0:T(128)} %param.9) | copy-start | bytes 1540
  85.3 3.9 %copy-start.2 = (bf16[512,512]{1,0:T(8,128)(2,1)}, bf16[512,512]{1,0:T(8,128)(2,1)S(1)}, u32[]{:S(2)}) copy-start(bf16[512,512]{1,0:T(8,128)(2,1)S(1)} %convolution_convert_fusion.1) | copy-start | bytes 1572868
  85.3 3.9 %collective-permute-start.3 = (bf16[512,512]{1,0:T(8,128)(2,1)S(1)}, bf16[512,512]{1,0:T(8,128)(2,1)}, u32[]{:S(2)}, u32[]{:S(2)}) collective-permute-start(bf16[512,512]{1,0:T(8,128)(2,1)S(1)} %convolution_convert_fusion.1), channel_id=1, source_target_pairs={{0,1},{1,0},{2,3},{3,2},{4,5},{5,4},{6,7},{7,6},{8,9},{9,8},{10,11... | collective-permute-start | bytes 1572872 | tf_op jit(solution)/shard_map/ppermute | solution.py:52
  92.7 31.2 %all-to-all-start.4 = ((bf16[16,32,1024]{2,1,0:T(8,128)(2,1)}), bf16[16,32,1024]{2,1,0:T(8,128)(2,1)S(1)}, u32[]{:S(2)}, u32[]{:S(2)}) async-start(bf16[16,32,1024]{2,1,0:T(8,128)(2,1)} %bitcast.42), calls=%async_computation.4 | async-start | bytes 2097152 | tf_op jit(solution)/shard_map/all_to_all | solution.py:13
  100.0 9.7 %collective-permute-start.4 = (bf16[128,1024]{1,0:T(8,128)(2,1)S(1)}, bf16[128,1024]{1,0:T(8,128)(2,1)S(1)}, u32[]{:S(2)}, u32[]{:S(2)}) collective-permute-start(bf16[128,1024]{1,0:T(8,128)(2,1)S(1)} %get-tuple-element.2), channel_id=1, source_target_pairs={{0,384},{128,0},{256,128},{384,256},{1,385},{129,1},{257,129},{385... | collective-permute-start | bytes 786440 | tf_op jit(solution)/shard_map/ppermute | solution.py:22
  103.1 16.2 %collective-permute-start.6 = (bf16[128,1024]{1,0:T(8,128)(2,1)S(1)}, bf16[128,1024]{1,0:T(8,128)(2,1)S(1)}, u32[]{:S(2)}, u32[]{:S(2)}) collective-permute-start(bf16[128,1024]{1,0:T(8,128)(2,1)S(1)} %get-tuple-element.3), channel_id=1, source_target_pairs={{0,128},{128,256},{256,384},{384,0},{1,129},{129,257},{257,385},{3... | collective-permute-start | bytes 786440 | tf_op jit(solution)/shard_map/ppermute | solution.py:22
  105.9 13.5 %collective-permute-start.5 = (bf16[128,1024]{1,0:T(8,128)(2,1)S(1)}, bf16[128,1024]{1,0:T(8,128)(2,1)S(1)}, u32[]{:S(2)}, u32[]{:S(2)}) collective-permute-start(bf16[128,1024]{1,0:T(8,128)(2,1)S(1)} %get-tuple-element.4), channel_id=1, source_target_pairs={{0,256},{128,384},{256,0},{384,128},{1,257},{129,385},{257,1},{385... | collective-permute-start | bytes 786440 | tf_op jit(solution)/shard_map/ppermute | solution.py:22

commit v5 on v4

--- a/solution.py
+++ b/solution.py
@@ -40,31 +40,31 @@
 
     q_send = jnp.broadcast_to(queries[None], (nzh, rows, cols))
     own = jnp.concatenate([q_send, passages.reshape(nzh, sub, cols)], axis=1)
-    own = exchange(own, "zh").transpose(1, 0, 2).reshape(rows + sub, nzh * cols)
-    q_own, p_own = own[:rows], own[rows:]
+    own = exchange(own, "zh")
+    p_own = lax.optimization_barrier(own[:, rows:].transpose(1, 0, 2)).reshape(sub, nzh * cols)
+    q_own = own[:, :rows].transpose(1, 0, 2).reshape(rows, nzh * cols)
 
     p_tile = exchange(jnp.broadcast_to(p_own[None], (blocks, sub, nzh * cols)), ("zl", "y"))
     p_tile = p_tile.reshape(blocks * sub, nzh * cols)
     q_tile = jnp.concatenate([q_own] + [shifted(q_own, "x", k) for k in range(1, nx)], axis=0)
-    q_tile = lax.optimization_barrier(q_tile)
 
-    part = dot(q_tile, p_tile, ((1,), (1,))).astype(BF16)
+    part = dot(p_tile, q_tile, ((1,), (1,))).astype(BF16)
     other = lax.ppermute(part, "core", [(0, 1), (1, 0)])
     scores = part.astype(F32) + other.astype(F32)
 
     own_block = lax.axis_index("zl") * ny + lax.axis_index("y")
     place = positive_index - lax.axis_index("zh") * sub
     target = jnp.where((place >= 0) & (place < sub), own_block * sub + place, -1)
-    target = jnp.pad(target, (0, (nx - 1) * rows), constant_values=-1)[:, None]
-    labels = (jnp.arange(blocks * sub, dtype=jnp.int32)[None, :] == target).astype(F32)
+    target = jnp.pad(target, (0, (nx - 1) * rows), constant_values=-1)[None, :]
+    labels = (jnp.arange(blocks * sub, dtype=jnp.int32)[:, None] == target).astype(F32)
     logits = scale_value * scores + bias_value
     weight = lax.optimization_barrier((jax.nn.sigmoid(logits) - labels).astype(BF16))
 
-    gp = dot(weight, q_tile, ((0,), (0,))).astype(BF16)
+    gp = dot(weight, q_tile, ((1,), (0,))).astype(BF16)
     gp = exchange(gp.reshape(blocks, sub, nzh * cols), ("zl", "y"))
     gp = jnp.sum(gp.astype(F32), axis=0)
 
-    gq = dot(weight, p_tile, ((1,), (0,)))
+    gq = dot(weight, p_tile, ((0,), (0,)))
     gq = gq[:rows] + sum(
         shifted(gq[k * rows : (k + 1) * rows].astype(BF16), "x", -k).astype(F32)
         for k in range(1, nx)

time: 142 us -> 141 us (level)
  no operation moved by 1% of the time
where the time goes in v5:
time: 141 us
  blocking collectives  69.1 us (49%)
  starting transfers between devices  31.6 us (22%)
  waiting for transfers between devices  28.3 us (20%)
  matrix products  4.89 us (3%)
  local copies, waits for them, and re-layouts  2.28 us (2%)
  other arithmetic  2.26 us (2%)
  between operations  2.18 us (2%)
    all_to_all x4, blocking collectives, exchange(): return lax.all_to_all(pieces, axes, 0, 0, tiled=True)  69.1 us
    ppermute x6, waiting for transfers between devices, shifted(): lax.ppermute(block, axis, [(i, (i + step) % size) for i in range(size)])  18.3 us
    ppermute x6, starting transfers between devices, shifted(): lax.ppermute(block, axis, [(i, (i + step) % size) for i in range(size)])  17 us
    all_to_all x2, starting transfers between devices, exchange(): return lax.all_to_all(pieces, axes, 0, 0, tiled=True)  12.7 us
    all_to_all x2, waiting for transfers between devices, exchange(): return lax.all_to_all(pieces, axes, 0, 0, tiled=True)  9.5 us
    dot_general x5, matrix products, dot(): lax.dot_general(left, right, (contract, ((), ())), preferred_element_type...  4.89 us
  transfers between devices with their start and end apart: 9, of which 8 were waited for; matrix products, arithmetic and copies ran while one was open for 1% of the time, Pallas kernels for 0%

profile of v5, /device:TPU:16, one launch (start us, length us, event | category | flops | bytes accessed | tf_op | source)
XLA Modules:
  0.0 140.6 jit_solution(3243183879510587786)
XLA Ops:
  0.6 0.8 broadcast_in_dim.16
  1.4 14.6 %all_to_all.30 = bf16[8,32,256]{2,1,0:T(8,128)(2,1)S(1)} all-to-all(bf16[8,32,256]{2,1,0:T(8,128)(2,1)S(1)} %broadcast_in_dim.16), channel_id=1, replica_groups=mesh['x'=4,'zl'=2,'y'=8,'zh'=4,'core'=2] {'y'}, dimensions={0} | all-to-all | bytes 262144 | tf_op jit(solution)/shard_map/all_to_all | solution.py:13
  16.2 19.3 %all_to_all.31 = bf16[8,256,256]{2,1,0:T(8,128)(2,1)S(1)} all-to-all(bf16[8,256,256]{2,1,0:T(8,128)(2,1)S(1)} %broadcast_in_dim.34), channel_id=1, replica_groups=mesh['x'=4,'zl'=2,'y'=8,'zh'=4,'core'=2] {'x','zl'}, dimensions={0} | all-to-all | bytes 2097152 | tf_op jit(solution)/shard_map/all_to_all | solution.py:13
  36.2 19.5 %all_to_all.32 = bf16[4,160,256]{2,1,0:T(8,128)(2,1)S(1)} all-to-all(bf16[4,160,256]{2,1,0:T(8,128)(2,1)S(1)} %pad_maximum_fusion.1), channel_id=1, replica_groups=mesh['x'=4,'zl'=2,'y'=8,'zh'=4,'core'=2] {'zh'}, dimensions={0} | all-to-all | bytes 655360 | tf_op jit(solution)/shard_map/all_to_all | solution.py:13
  55.7 1.1 broadcast_in_dim.37
  56.8 6.1 %all-to-all-start.3 = ((bf16[16,32,1024]{2,1,0:T(8,128)(2,1)}), bf16[16,32,1024]{2,1,0:T(8,128)(2,1)S(1)}, u32[]{:S(2)}, u32[]{:S(2)}) async-start(bf16[16,32,1024]{2,1,0:T(8,128)(2,1)} %broadcast_in_dim.37), calls=%async_computation.3 | async-start | bytes 2097152 | tf_op jit(solution)/shard_map/all_to_all | solution.py:13
  63.1 3.1 %collective-permute-start.2 = (bf16[128,1024]{0,1:T(8,128)(2,1)S(1)}, bf16[128,1024]{0,1:T(8,128)(2,1)S(1)}, u32[]{:S(2)}, u32[]{:S(2)}) collective-permute-start(bf16[128,1024]{0,1:T(8,128)(2,1)S(1)} %bitcast.49), channel_id=1, source_target_pairs={{0,384},{128,0},{256,128},{384,256},{1,385},{129,1},{257,129},{385... | collective-permute-start | bytes 786440 | tf_op jit(solution)/shard_map/ppermute | solution.py:22
  66.1 3.0 %collective-permute-start.1 = (bf16[128,1024]{0,1:T(8,128)(2,1)S(1)}, bf16[128,1024]{0,1:T(8,128)(2,1)S(1)}, u32[]{:S(2)}, u32[]{:S(2)}) collective-permute-start(bf16[128,1024]{0,1:T(8,128)(2,1)S(1)} %bitcast.50), channel_id=1, source_target_pairs={{0,256},{128,384},{256,0},{384,128},{1,257},{129,385},{257,1},{385... | collective-permute-start | bytes 786440 | tf_op jit(solution)/shard_map/ppermute | solution.py:22
  69.2 2.1 %collective-permute-start = (bf16[128,1024]{0,1:T(8,128)(2,1)S(1)}, bf16[128,1024]{0,1:T(8,128)(2,1)S(1)}, u32[]{:S(2)}, u32[]{:S(2)}) collective-permute-start(bf16[128,1024]{0,1:T(8,128)(2,1)S(1)} %bitcast.51), channel_id=1, source_target_pairs={{0,128},{128,256},{256,384},{384,0},{1,129},{129,257},{257,385},{3... | collective-permute-start | bytes 786440 | tf_op jit(solution)/shard_map/ppermute | solution.py:22
  71.6 4.6 %collective-permute-done.1 = bf16[128,1024]{0,1:T(8,128)(2,1)S(1)} collective-permute-done((bf16[128,1024]{0,1:T(8,128)(2,1)S(1)}, bf16[128,1024]{0,1:T(8,128)(2,1)S(1)}, u32[]{:S(2)}, u32[]{:S(2)}) %collective-permute-start.1) | collective-permute-done | bytes 262176 | tf_op jit(solution)/shard_map/ppermute | solution.py:22
  76.3 2.8 %collective-permute-done = bf16[128,1024]{0,1:T(8,128)(2,1)S(1)} collective-permute-done((bf16[128,1024]{0,1:T(8,128)(2,1)S(1)}, bf16[128,1024]{0,1:T(8,128)(2,1)S(1)}, u32[]{:S(2)}, u32[]{:S(2)}) %collective-permute-start) | collective-permute-done | bytes 262176 | tf_op jit(solution)/shard_map/ppermute | solution.py:22
  79.1 5.1 %all-to-all-done.3 = bf16[16,32,1024]{2,1,0:T(8,128)(2,1)S(1)} async-done(((bf16[16,32,1024]{2,1,0:T(8,128)(2,1)}), bf16[16,32,1024]{2,1,0:T(8,128)(2,1)S(1)}, u32[]{:S(2)}, u32[]{:S(2)}) %all-to-all-start.3) | async-done | bytes 1048608 | tf_op jit(solution)/shard_map/all_to_all | solution.py:13
  84.2 0.7 convolution_convert_fusion.1
  84.9 1.9 %collective-permute-start.3 = (bf16[512,512]{1,0:T(8,128)(2,1)S(1)}, bf16[512,512]{1,0:T(8,128)(2,1)S(1)}, u32[]{:S(2)}, u32[]{:S(2)}) collective-permute-start(bf16[512,512]{1,0:T(8,128)(2,1)S(1)} %convolution_convert_fusion.1), channel_id=1, source_target_pairs={{0,1},{1,0},{2,3},{3,2},{4,5},{5,4},{6,7},{7,6},{8,9},{9,8},{10,11... | collective-permute-start | bytes 1572872 | tf_op jit(solution)/shard_map/ppermute | solution.py:52
  89.2 2.8 %convolution_convert_fusion = bf16[512,1024]{1,0:T(8,128)(2,1)} fusion(bf16[512,512]{1,0:T(8,128)(2,1)S(1)} %subtract_convert_fusion, bf16[128,1024]{0,1:T(8,128)(2,1)} %copy-done.3, bf16[128,1024]{0,1:T(8,128)(2,1)} %copy-done.4, bf16[128,1024]{0,1:T(8,128)(2,1)} %copy-done.5, bf16[128,1024]{0,1:T(8,128)(2,1)S(1)} %bitcast.53), kind=kOutput, calls=%fused_computation | convolution fusion | flops 541589504 | bytes 2621440 | tf_op jit(solution)/shard_map/dot_general | solution.py:17
  92.0 6.5 %all-to-all-start.4 = ((bf16[16,32,1024]{2,1,0:T(8,128)(2,1)}), bf16[16,32,1024]{2,1,0:T(8,128)(2,1)S(1)}, u32[]{:S(2)}, u32[]{:S(2)}) async-start(bf16[16,32,1024]{2,1,0:T(8,128)(2,1)} %bitcast.41), calls=%async_computation.4 | async-start | bytes 2097152 | tf_op jit(solution)/shard_map/all_to_all | solution.py:13
  98.6 0.7 fusion.4
  99.4 3.1 %collective-permute-start.4 = (bf16[128,1024]{1,0:T(8,128)(2,1)S(1)}, bf16[128,1024]{1,0:T(8,128)(2,1)S(1)}, u32[]{:S(2)}, u32[]{:S(2)}) collective-permute-start(bf16[128,1024]{1,0:T(8,128)(2,1)S(1)} %get-tuple-element.2), channel_id=1, source_target_pairs={{0,384},{128,0},{256,128},{384,256},{1,385},{129,1},{257,129},{385... | collective-permute-start | bytes 786440 | tf_op jit(solution)/shard_map/ppermute | solution.py:22
  102.5 2.7 %collective-permute-start.6 = (bf16[128,1024]{1,0:T(8,128)(2,1)S(1)}, bf16[128,1024]{1,0:T(8,128)(2,1)S(1)}, u32[]{:S(2)}, u32[]{:S(2)}) collective-permute-start(bf16[128,1024]{1,0:T(8,128)(2,1)S(1)} %get-tuple-element.3), channel_id=1, source_target_pairs={{0,128},{128,256},{256,384},{384,0},{1,129},{129,257},{257,385},{3... | collective-permute-start | bytes 786440 | tf_op jit(solution)/shard_map/ppermute | solution.py:22
  105.2 3.0 %collective-permute-start.5 = (bf16[128,1024]{1,0:T(8,128)(2,1)S(1)}, bf16[128,1024]{1,0:T(8,128)(2,1)S(1)}, u32[]{:S(2)}, u32[]{:S(2)}) collective-permute-start(bf16[128,1024]{1,0:T(8,128)(2,1)S(1)} %get-tuple-element.4), channel_id=1, source_target_pairs={{0,256},{128,384},{256,0},{384,128},{1,257},{129,385},{257,1},{385... | collective-permute-start | bytes 786440 | tf_op jit(solution)/shard_map/ppermute | solution.py:22
  108.2 0.8 collective-permute-done.4
  109.1 9.7 %collective-permute-done.6 = bf16[128,1024]{1,0:T(8,128)(2,1)S(1)} collective-permute-done((bf16[128,1024]{1,0:T(8,128)(2,1)S(1)}, bf16[128,1024]{1,0:T(8,128)(2,1)S(1)}, u32[]{:S(2)}, u32[]{:S(2)}) %collective-permute-start.6) | collective-permute-done | bytes 262176 | tf_op jit(solution)/shard_map/ppermute | solution.py:22
  118.9 4.4 %all-to-all-done.4 = bf16[16,32,1024]{2,1,0:T(8,128)(2,1)S(1)} async-done(((bf16[16,32,1024]{2,1,0:T(8,128)(2,1)}), bf16[16,32,1024]{2,1,0:T(8,128)(2,1)S(1)}, u32[]{:S(2)}, u32[]{:S(2)}) %all-to-all-start.4) | async-done | bytes 1048608 | tf_op jit(solution)/shard_map/all_to_all | solution.py:13
  123.5 15.7 %all_to_all.33 = bf16[4,160,256]{2,1,0:T(8,128)(2,1)S(1)} all-to-all(bf16[4,160,256]{2,1,0:T(8,128)(2,1)S(1)} %maximum_bitcast_fusion), channel_id=1, replica_groups=mesh['x'=4,'zl'=2,'y'=8,'zh'=4,'core'=2] {'zh'}, dimensions={0} | all-to-all | bytes 655360 | tf_op jit(solution)/shard_map/all_to_all | solution.py:13
  (37 shorter events, 4.2 us)
Async XLA Ops:
  0.6 34.8 %copy-start = (bf16[128,2048]{1,0:T(8,128)(2,1)S(1)}, bf16[128,2048]{1,0:T(8,128)(2,1)}, u32[]{:S(2)}) copy-start(bf16[128,2048]{1,0:T(8,128)(2,1)} %param.7) | copy-start | bytes 1572868
  16.1 19.6 %copy-start.1 = (bf16[128,2048]{1,0:T(8,128)(2,1)S(1)}, bf16[128,2048]{1,0:T(8,128)(2,1)}, u32[]{:S(2)}) copy-start(bf16[128,2048]{1,0:T(8,128)(2,1)} %param.6) | copy-start | bytes 1572868
  56.8 27.4 %all-to-all-start.3 = ((bf16[16,32,1024]{2,1,0:T(8,128)(2,1)}), bf16[16,32,1024]{2,1,0:T(8,128)(2,1)S(1)}, u32[]{:S(2)}, u32[]{:S(2)}) async-start(bf16[16,32,1024]{2,1,0:T(8,128)(2,1)} %broadcast_in_dim.37), calls=%async_computation.3 | async-start | bytes 2097152 | tf_op jit(solution)/shard_map/all_to_all | solution.py:13
  63.1 8.6 %collective-permute-start.2 = (bf16[128,1024]{0,1:T(8,128)(2,1)S(1)}, bf16[128,1024]{0,1:T(8,128)(2,1)S(1)}, u32[]{:S(2)}, u32[]{:S(2)}) collective-permute-start(bf16[128,1024]{0,1:T(8,128)(2,1)S(1)} %bitcast.49), channel_id=1, source_target_pairs={{0,384},{128,0},{256,128},{384,256},{1,385},{129,1},{257,129},{385... | collective-permute-start | bytes 786440 | tf_op jit(solution)/shard_map/ppermute | solution.py:22
  66.1 10.1 %collective-permute-start.1 = (bf16[128,1024]{0,1:T(8,128)(2,1)S(1)}, bf16[128,1024]{0,1:T(8,128)(2,1)S(1)}, u32[]{:S(2)}, u32[]{:S(2)}) collective-permute-start(bf16[128,1024]{0,1:T(8,128)(2,1)S(1)} %bitcast.50), channel_id=1, source_target_pairs={{0,256},{128,384},{256,0},{384,128},{1,257},{129,385},{257,1},{385... | collective-permute-start | bytes 786440 | tf_op jit(solution)/shard_map/ppermute | solution.py:22
  69.2 9.9 %collective-permute-start = (bf16[128,1024]{0,1:T(8,128)(2,1)S(1)}, bf16[128,1024]{0,1:T(8,128)(2,1)S(1)}, u32[]{:S(2)}, u32[]{:S(2)}) collective-permute-start(bf16[128,1024]{0,1:T(8,128)(2,1)S(1)} %bitcast.51), channel_id=1, source_target_pairs={{0,128},{128,256},{256,384},{384,0},{1,129},{129,257},{257,385},{3... | collective-permute-start | bytes 786440 | tf_op jit(solution)/shard_map/ppermute | solution.py:22
  71.6 12.6 %copy-start.3 = (bf16[128,1024]{0,1:T(8,128)(2,1)}, bf16[128,1024]{0,1:T(8,128)(2,1)S(1)}, u32[]{:S(2)}) copy-start(bf16[128,1024]{0,1:T(8,128)(2,1)S(1)} %collective-permute-done.2) | copy-start | bytes 786436
  76.3 7.9 %copy-start.4 = (bf16[128,1024]{0,1:T(8,128)(2,1)}, bf16[128,1024]{0,1:T(8,128)(2,1)S(1)}, u32[]{:S(2)}) copy-start(bf16[128,1024]{0,1:T(8,128)(2,1)S(1)} %collective-permute-done.1) | copy-start | bytes 786436
  79.1 5.9 %copy-start.5 = (bf16[128,1024]{0,1:T(8,128)(2,1)}, bf16[128,1024]{0,1:T(8,128)(2,1)S(1)}, u32[]{:S(2)}) copy-start(bf16[128,1024]{0,1:T(8,128)(2,1)S(1)} %collective-permute-done) | copy-start | bytes 786436
  84.2 4.0 %copy-start.2 = (s32[128]{0:T(128)S(1)}, s32[128]{0:T(128)}, u32[]{:S(2)}) copy-start(s32[128]{0:T(128)} %param.9) | copy-start | bytes 1540
  84.9 3.8 %collective-permute-start.3 = (bf16[512,512]{1,0:T(8,128)(2,1)S(1)}, bf16[512,512]{1,0:T(8,128)(2,1)S(1)}, u32[]{:S(2)}, u32[]{:S(2)}) collective-permute-start(bf16[512,512]{1,0:T(8,128)(2,1)S(1)} %convolution_convert_fusion.1), channel_id=1, source_target_pairs={{0,1},{1,0},{2,3},{3,2},{4,5},{5,4},{6,7},{7,6},{8,9},{9,8},{10,11... | collective-permute-start | bytes 1572872 | tf_op jit(solution)/shard_map/ppermute | solution.py:52
  92.0 31.2 %all-to-all-start.4 = ((bf16[16,32,1024]{2,1,0:T(8,128)(2,1)}), bf16[16,32,1024]{2,1,0:T(8,128)(2,1)S(1)}, u32[]{:S(2)}, u32[]{:S(2)}) async-start(bf16[16,32,1024]{2,1,0:T(8,128)(2,1)} %bitcast.41), calls=%async_computation.4 | async-start | bytes 2097152 | tf_op jit(solution)/shard_map/all_to_all | solution.py:13
  99.4 9.7 %collective-permute-start.4 = (bf16[128,1024]{1,0:T(8,128)(2,1)S(1)}, bf16[128,1024]{1,0:T(8,128)(2,1)S(1)}, u32[]{:S(2)}, u32[]{:S(2)}) collective-permute-start(bf16[128,1024]{1,0:T(8,128)(2,1)S(1)} %get-tuple-element.2), channel_id=1, source_target_pairs={{0,384},{128,0},{256,128},{384,256},{1,385},{129,1},{257,129},{385... | collective-permute-start | bytes 786440 | tf_op jit(solution)/shard_map/ppermute | solution.py:22
  102.5 16.2 %collective-permute-start.6 = (bf16[128,1024]{1,0:T(8,128)(2,1)S(1)}, bf16[128,1024]{1,0:T(8,128)(2,1)S(1)}, u32[]{:S(2)}, u32[]{:S(2)}) collective-permute-start(bf16[128,1024]{1,0:T(8,128)(2,1)S(1)} %get-tuple-element.3), channel_id=1, source_target_pairs={{0,128},{128,256},{256,384},{384,0},{1,129},{129,257},{257,385},{3... | collective-permute-start | bytes 786440 | tf_op jit(solution)/shard_map/ppermute | solution.py:22
  105.2 13.5 %collective-permute-start.5 = (bf16[128,1024]{1,0:T(8,128)(2,1)S(1)}, bf16[128,1024]{1,0:T(8,128)(2,1)S(1)}, u32[]{:S(2)}, u32[]{:S(2)}) collective-permute-start(bf16[128,1024]{1,0:T(8,128)(2,1)S(1)} %get-tuple-element.4), channel_id=1, source_target_pairs={{0,256},{128,384},{256,0},{384,128},{1,257},{129,385},{257,1},{385... | collective-permute-start | bytes 786440 | tf_op jit(solution)/shard_map/ppermute | solution.py:22

commit v6 on v5

--- a/solution.py
+++ b/solution.py
@@ -1,6 +1,8 @@
 import jax
 import jax.numpy as jnp
 from jax import lax
+from jax.experimental import pallas as pl
+from jax.experimental.pallas import tpu as pltpu
 from jax.sharding import Mesh, PartitionSpec as P
 
 BF16 = jnp.bfloat16
@@ -20,6 +22,12 @@
 def shifted(block, axis, step):
     size = lax.axis_size(axis)
     return lax.ppermute(block, axis, [(i, (i + step) % size) for i in range(size)])
+
+
+def finish_kernel(scale, both, grad_q, grad_p):
+    rows = grad_q.shape[0]
+    grad_q[...] = scale[0] * jnp.sum(both[:, :rows].astype(F32), axis=0)
+    grad_p[...] = (scale[0] * both[:, rows:].astype(F32)).reshape(grad_p.shape)
 
 
 def per_device(query_states, passage_states, proj_weight, positive_index, logit_scale, logit_bias):
@@ -71,10 +79,16 @@
     )
 
     both = jnp.concatenate([gq, gp], axis=0).astype(BF16).reshape(rows + sub, nzh, cols)
-    both = exchange(both.transpose(1, 0, 2), "zh").astype(F32)
-    grad_q = jnp.sum(both[:, :rows], axis=0)
-    grad_p = both[:, rows:].reshape(rows, cols)
-    return (scale_value * grad_q, scale_value * grad_p)
+    both = exchange(both.transpose(1, 0, 2), "zh")
+    return pl.pallas_call(
+        finish_kernel,
+        in_specs=[
+            pl.BlockSpec(memory_space=pltpu.SMEM),
+            pl.BlockSpec(memory_space=pltpu.VMEM),
+        ],
+        out_shape=[jax.ShapeDtypeStruct((rows, cols), F32)] * 2,
+        compiler_params=pltpu.CompilerParams(vmem_limit_bytes=8 * 1024 * 1024),
+    )(logit_scale, both)
 
 
 def solution(mesh):

time: 141 us -> 141 us (level)
  no operation moved by 1% of the time
where the time goes in v6:
time: 141 us; the launch traced here: 140 us
  blocking collectives  69.1 us (49%)
  starting transfers between devices  31.6 us (22%)
  waiting for transfers between devices  28 us (20%)
  matrix products  4.89 us (3%)
  local copies, waits for them, and re-layouts  2.59 us (2%)
  between operations  2.17 us (2%)
    all_to_all x4, blocking collectives, exchange(): return lax.all_to_all(pieces, axes, 0, 0, tiled=True)  69.1 us
    ppermute x6, waiting for transfers between devices, shifted(): lax.ppermute(block, axis, [(i, (i + step) % size) for i in range(size)])  18.3 us
    ppermute x6, starting transfers between devices, shifted(): lax.ppermute(block, axis, [(i, (i + step) % size) for i in range(size)])  17 us
    all_to_all x2, starting transfers between devices, exchange(): return lax.all_to_all(pieces, axes, 0, 0, tiled=True)  12.7 us
    all_to_all x2, waiting for transfers between devices, exchange(): return lax.all_to_all(pieces, axes, 0, 0, tiled=True)  9.19 us
    dot_general x5, matrix products, dot(): lax.dot_general(left, right, (contract, ((), ())), preferred_element_type...  4.89 us
  transfers between devices with their start and end apart: 9, of which 8 were waited for; matrix products, arithmetic and copies ran while one was open for 1% of the time, Pallas kernels for 0%

profile of v6, /device:TPU:16, one launch (start us, length us, event | category | flops | bytes accessed | tf_op | source)
XLA Modules:
  0.0 140.0 jit_solution(5890099154954556819)
XLA Ops:
  0.6 0.8 broadcast_in_dim.16
  1.4 14.6 %all_to_all.30 = bf16[8,32,256]{2,1,0:T(8,128)(2,1)S(1)} all-to-all(bf16[8,32,256]{2,1,0:T(8,128)(2,1)S(1)} %broadcast_in_dim.16), channel_id=1, replica_groups=mesh['x'=4,'zl'=2,'y'=8,'zh'=4,'core'=2] {'y'}, dimensions={0} | all-to-all | bytes 262144 | tf_op jit(solution)/shard_map/all_to_all | solution.py:15
  16.2 19.3 %all_to_all.31 = bf16[8,256,256]{2,1,0:T(8,128)(2,1)S(1)} all-to-all(bf16[8,256,256]{2,1,0:T(8,128)(2,1)S(1)} %broadcast_in_dim.34), channel_id=1, replica_groups=mesh['x'=4,'zl'=2,'y'=8,'zh'=4,'core'=2] {'x','zl'}, dimensions={0} | all-to-all | bytes 2097152 | tf_op jit(solution)/shard_map/all_to_all | solution.py:15
  36.2 19.5 %all_to_all.32 = bf16[4,160,256]{2,1,0:T(8,128)(2,1)S(1)} all-to-all(bf16[4,160,256]{2,1,0:T(8,128)(2,1)S(1)} %pad_maximum_fusion.1), channel_id=1, replica_groups=mesh['x'=4,'zl'=2,'y'=8,'zh'=4,'core'=2] {'zh'}, dimensions={0} | all-to-all | bytes 655360 | tf_op jit(solution)/shard_map/all_to_all | solution.py:15
  55.7 1.1 broadcast_in_dim.37
  56.8 6.1 %all-to-all-start.3 = ((bf16[16,32,1024]{2,1,0:T(8,128)(2,1)}), bf16[16,32,1024]{2,1,0:T(8,128)(2,1)S(1)}, u32[]{:S(2)}, u32[]{:S(2)}) async-start(bf16[16,32,1024]{2,1,0:T(8,128)(2,1)} %broadcast_in_dim.37), calls=%async_computation.3 | async-start | bytes 2097152 | tf_op jit(solution)/shard_map/all_to_all | solution.py:15
  63.1 3.1 %collective-permute-start.2 = (bf16[128,1024]{0,1:T(8,128)(2,1)S(1)}, bf16[128,1024]{0,1:T(8,128)(2,1)S(1)}, u32[]{:S(2)}, u32[]{:S(2)}) collective-permute-start(bf16[128,1024]{0,1:T(8,128)(2,1)S(1)} %bitcast.42), channel_id=1, source_target_pairs={{0,384},{128,0},{256,128},{384,256},{1,385},{129,1},{257,129},{385... | collective-permute-start | bytes 786440 | tf_op jit(solution)/shard_map/ppermute | solution.py:24
  66.1 3.0 %collective-permute-start.1 = (bf16[128,1024]{0,1:T(8,128)(2,1)S(1)}, bf16[128,1024]{0,1:T(8,128)(2,1)S(1)}, u32[]{:S(2)}, u32[]{:S(2)}) collective-permute-start(bf16[128,1024]{0,1:T(8,128)(2,1)S(1)} %bitcast.43), channel_id=1, source_target_pairs={{0,256},{128,384},{256,0},{384,128},{1,257},{129,385},{257,1},{385... | collective-permute-start | bytes 786440 | tf_op jit(solution)/shard_map/ppermute | solution.py:24
  69.2 2.1 %collective-permute-start = (bf16[128,1024]{0,1:T(8,128)(2,1)S(1)}, bf16[128,1024]{0,1:T(8,128)(2,1)S(1)}, u32[]{:S(2)}, u32[]{:S(2)}) collective-permute-start(bf16[128,1024]{0,1:T(8,128)(2,1)S(1)} %bitcast.44), channel_id=1, source_target_pairs={{0,128},{128,256},{256,384},{384,0},{1,129},{129,257},{257,385},{3... | collective-permute-start | bytes 786440 | tf_op jit(solution)/shard_map/ppermute | solution.py:24
  71.7 4.6 %collective-permute-done.1 = bf16[128,1024]{0,1:T(8,128)(2,1)S(1)} collective-permute-done((bf16[128,1024]{0,1:T(8,128)(2,1)S(1)}, bf16[128,1024]{0,1:T(8,128)(2,1)S(1)}, u32[]{:S(2)}, u32[]{:S(2)}) %collective-permute-start.1) | collective-permute-done | bytes 262176 | tf_op jit(solution)/shard_map/ppermute | solution.py:24
  76.3 2.8 %collective-permute-done = bf16[128,1024]{0,1:T(8,128)(2,1)S(1)} collective-permute-done((bf16[128,1024]{0,1:T(8,128)(2,1)S(1)}, bf16[128,1024]{0,1:T(8,128)(2,1)S(1)}, u32[]{:S(2)}, u32[]{:S(2)}) %collective-permute-start) | collective-permute-done | bytes 262176 | tf_op jit(solution)/shard_map/ppermute | solution.py:24
  79.1 5.1 %all-to-all-done.3 = bf16[16,32,1024]{2,1,0:T(8,128)(2,1)S(1)} async-done(((bf16[16,32,1024]{2,1,0:T(8,128)(2,1)}), bf16[16,32,1024]{2,1,0:T(8,128)(2,1)S(1)}, u32[]{:S(2)}, u32[]{:S(2)}) %all-to-all-start.3) | async-done | bytes 1048608 | tf_op jit(solution)/shard_map/all_to_all | solution.py:15
  84.9 1.9 %collective-permute-start.3 = (bf16[512,512]{1,0:T(8,128)(2,1)S(1)}, bf16[512,512]{1,0:T(8,128)(2,1)S(1)}, u32[]{:S(2)}, u32[]{:S(2)}) collective-permute-start(bf16[512,512]{1,0:T(8,128)(2,1)S(1)} %convolution_convert_fusion.1), channel_id=1, source_target_pairs={{0,1},{1,0},{2,3},{3,2},{4,5},{5,4},{6,7},{7,6},{8,9},{9,8},{10,11... | collective-permute-start | bytes 1572872 | tf_op jit(solution)/shard_map/ppermute | solution.py:60
  89.2 2.8 %convolution_convert_fusion = bf16[512,1024]{1,0:T(8,128)(2,1)} fusion(bf16[512,512]{1,0:T(8,128)(2,1)S(1)} %subtract_convert_fusion, bf16[128,1024]{0,1:T(8,128)(2,1)} %copy-done.3, bf16[128,1024]{0,1:T(8,128)(2,1)} %copy-done.4, bf16[128,1024]{0,1:T(8,128)(2,1)} %copy-done.5, bf16[128,1024]{0,1:T(8,128)(2,1)S(1)} %bitcast.46), kind=kOutput, calls=%fused_computation | convolution fusion | flops 541589504 | bytes 2621440 | tf_op jit(solution)/shard_map/dot_general | solution.py:19
  92.0 6.6 %all-to-all-start.4 = ((bf16[16,32,1024]{2,1,0:T(8,128)(2,1)}), bf16[16,32,1024]{2,1,0:T(8,128)(2,1)S(1)}, u32[]{:S(2)}, u32[]{:S(2)}) async-start(bf16[16,32,1024]{2,1,0:T(8,128)(2,1)} %bitcast.35), calls=%async_computation.4 | async-start | bytes 2097152 | tf_op jit(solution)/shard_map/all_to_all | solution.py:15
  98.6 0.7 fusion.4
  99.4 3.1 %collective-permute-start.4 = (bf16[128,1024]{1,0:T(8,128)(2,1)S(1)}, bf16[128,1024]{1,0:T(8,128)(2,1)S(1)}, u32[]{:S(2)}, u32[]{:S(2)}) collective-permute-start(bf16[128,1024]{1,0:T(8,128)(2,1)S(1)} %get-tuple-element.2), channel_id=1, source_target_pairs={{0,384},{128,0},{256,128},{384,256},{1,385},{129,1},{257,129},{385... | collective-permute-start | bytes 786440 | tf_op jit(solution)/shard_map/ppermute | solution.py:24
  102.5 2.7 %collective-permute-start.6 = (bf16[128,1024]{1,0:T(8,128)(2,1)S(1)}, bf16[128,1024]{1,0:T(8,128)(2,1)S(1)}, u32[]{:S(2)}, u32[]{:S(2)}) collective-permute-start(bf16[128,1024]{1,0:T(8,128)(2,1)S(1)} %get-tuple-element.3), channel_id=1, source_target_pairs={{0,128},{128,256},{256,384},{384,0},{1,129},{129,257},{257,385},{3... | collective-permute-start | bytes 786440 | tf_op jit(solution)/shard_map/ppermute | solution.py:24
  105.2 3.0 %collective-permute-start.5 = (bf16[128,1024]{1,0:T(8,128)(2,1)S(1)}, bf16[128,1024]{1,0:T(8,128)(2,1)S(1)}, u32[]{:S(2)}, u32[]{:S(2)}) collective-permute-start(bf16[128,1024]{1,0:T(8,128)(2,1)S(1)} %get-tuple-element.4), channel_id=1, source_target_pairs={{0,256},{128,384},{256,0},{384,128},{1,257},{129,385},{257,1},{385... | collective-permute-start | bytes 786440 | tf_op jit(solution)/shard_map/ppermute | solution.py:24
  108.2 0.8 collective-permute-done.4
  109.1 9.7 %collective-permute-done.6 = bf16[128,1024]{1,0:T(8,128)(2,1)S(1)} collective-permute-done((bf16[128,1024]{1,0:T(8,128)(2,1)S(1)}, bf16[128,1024]{1,0:T(8,128)(2,1)S(1)}, u32[]{:S(2)}, u32[]{:S(2)}) %collective-permute-start.6) | collective-permute-done | bytes 262176 | tf_op jit(solution)/shard_map/ppermute | solution.py:24
  119.2 4.1 %all-to-all-done.4 = bf16[16,32,1024]{2,1,0:T(8,128)(2,1)S(1)} async-done(((bf16[16,32,1024]{2,1,0:T(8,128)(2,1)}), bf16[16,32,1024]{2,1,0:T(8,128)(2,1)S(1)}, u32[]{:S(2)}, u32[]{:S(2)}) %all-to-all-start.4) | async-done | bytes 1048608 | tf_op jit(solution)/shard_map/all_to_all | solution.py:15
  123.5 15.7 %all_to_all.33.both = bf16[4,160,256]{2,1,0:T(8,128)(2,1)S(1)} all-to-all(bf16[4,160,256]{2,1,0:T(8,128)(2,1)S(1)} %maximum_bitcast_fusion), channel_id=1, replica_groups=mesh['x'=4,'zl'=2,'y'=8,'zh'=4,'core'=2] {'zh'}, dimensions={0} | all-to-all | bytes 655360 | tf_op jit(solution)/shard_map/all_to_all | solution.py:15
  139.2 0.7 shard_map.77
  (35 shorter events, 3.8 us)
Async XLA Ops:
  0.6 34.8 %copy-start = (bf16[128,2048]{1,0:T(8,128)(2,1)S(1)}, bf16[128,2048]{1,0:T(8,128)(2,1)}, u32[]{:S(2)}) copy-start(bf16[128,2048]{1,0:T(8,128)(2,1)} %param.7) | copy-start | bytes 1572868
  16.1 19.6 %copy-start.1 = (bf16[128,2048]{1,0:T(8,128)(2,1)S(1)}, bf16[128,2048]{1,0:T(8,128)(2,1)}, u32[]{:S(2)}) copy-start(bf16[128,2048]{1,0:T(8,128)(2,1)} %param.6) | copy-start | bytes 1572868
  56.8 27.4 %all-to-all-start.3 = ((bf16[16,32,1024]{2,1,0:T(8,128)(2,1)}), bf16[16,32,1024]{2,1,0:T(8,128)(2,1)S(1)}, u32[]{:S(2)}, u32[]{:S(2)}) async-start(bf16[16,32,1024]{2,1,0:T(8,128)(2,1)} %broadcast_in_dim.37), calls=%async_computation.3 | async-start | bytes 2097152 | tf_op jit(solution)/shard_map/all_to_all | solution.py:15
  63.1 8.6 %collective-permute-start.2 = (bf16[128,1024]{0,1:T(8,128)(2,1)S(1)}, bf16[128,1024]{0,1:T(8,128)(2,1)S(1)}, u32[]{:S(2)}, u32[]{:S(2)}) collective-permute-start(bf16[128,1024]{0,1:T(8,128)(2,1)S(1)} %bitcast.42), channel_id=1, source_target_pairs={{0,384},{128,0},{256,128},{384,256},{1,385},{129,1},{257,129},{385... | collective-permute-start | bytes 786440 | tf_op jit(solution)/shard_map/ppermute | solution.py:24
  66.1 10.1 %collective-permute-start.1 = (bf16[128,1024]{0,1:T(8,128)(2,1)S(1)}, bf16[128,1024]{0,1:T(8,128)(2,1)S(1)}, u32[]{:S(2)}, u32[]{:S(2)}) collective-permute-start(bf16[128,1024]{0,1:T(8,128)(2,1)S(1)} %bitcast.43), channel_id=1, source_target_pairs={{0,256},{128,384},{256,0},{384,128},{1,257},{129,385},{257,1},{385... | collective-permute-start | bytes 786440 | tf_op jit(solution)/shard_map/ppermute | solution.py:24
  69.2 9.9 %collective-permute-start = (bf16[128,1024]{0,1:T(8,128)(2,1)S(1)}, bf16[128,1024]{0,1:T(8,128)(2,1)S(1)}, u32[]{:S(2)}, u32[]{:S(2)}) collective-permute-start(bf16[128,1024]{0,1:T(8,128)(2,1)S(1)} %bitcast.44), channel_id=1, source_target_pairs={{0,128},{128,256},{256,384},{384,0},{1,129},{129,257},{257,385},{3... | collective-permute-start | bytes 786440 | tf_op jit(solution)/shard_map/ppermute | solution.py:24
  71.6 12.6 %copy-start.3 = (bf16[128,1024]{0,1:T(8,128)(2,1)}, bf16[128,1024]{0,1:T(8,128)(2,1)S(1)}, u32[]{:S(2)}) copy-start(bf16[128,1024]{0,1:T(8,128)(2,1)S(1)} %collective-permute-done.2) | copy-start | bytes 786436
  76.3 7.9 %copy-start.4 = (bf16[128,1024]{0,1:T(8,128)(2,1)}, bf16[128,1024]{0,1:T(8,128)(2,1)S(1)}, u32[]{:S(2)}) copy-start(bf16[128,1024]{0,1:T(8,128)(2,1)S(1)} %collective-permute-done.1) | copy-start | bytes 786436
  79.1 5.9 %copy-start.5 = (bf16[128,1024]{0,1:T(8,128)(2,1)}, bf16[128,1024]{0,1:T(8,128)(2,1)S(1)}, u32[]{:S(2)}) copy-start(bf16[128,1024]{0,1:T(8,128)(2,1)S(1)} %collective-permute-done) | copy-start | bytes 786436
  84.2 4.0 %copy-start.2 = (s32[128]{0:T(128)S(1)}, s32[128]{0:T(128)}, u32[]{:S(2)}) copy-start(s32[128]{0:T(128)} %param.9) | copy-start | bytes 1540
  84.9 3.8 %collective-permute-start.3 = (bf16[512,512]{1,0:T(8,128)(2,1)S(1)}, bf16[512,512]{1,0:T(8,128)(2,1)S(1)}, u32[]{:S(2)}, u32[]{:S(2)}) collective-permute-start(bf16[512,512]{1,0:T(8,128)(2,1)S(1)} %convolution_convert_fusion.1), channel_id=1, source_target_pairs={{0,1},{1,0},{2,3},{3,2},{4,5},{5,4},{6,7},{7,6},{8,9},{9,8},{10,11... | collective-permute-start | bytes 1572872 | tf_op jit(solution)/shard_map/ppermute | solution.py:60
  92.0 31.2 %all-to-all-start.4 = ((bf16[16,32,1024]{2,1,0:T(8,128)(2,1)}), bf16[16,32,1024]{2,1,0:T(8,128)(2,1)S(1)}, u32[]{:S(2)}, u32[]{:S(2)}) async-start(bf16[16,32,1024]{2,1,0:T(8,128)(2,1)} %bitcast.35), calls=%async_computation.4 | async-start | bytes 2097152 | tf_op jit(solution)/shard_map/all_to_all | solution.py:15
  99.4 9.7 %collective-permute-start.4 = (bf16[128,1024]{1,0:T(8,128)(2,1)S(1)}, bf16[128,1024]{1,0:T(8,128)(2,1)S(1)}, u32[]{:S(2)}, u32[]{:S(2)}) collective-permute-start(bf16[128,1024]{1,0:T(8,128)(2,1)S(1)} %get-tuple-element.2), channel_id=1, source_target_pairs={{0,384},{128,0},{256,128},{384,256},{1,385},{129,1},{257,129},{385... | collective-permute-start | bytes 786440 | tf_op jit(solution)/shard_map/ppermute | solution.py:24
  102.5 16.2 %collective-permute-start.6 = (bf16[128,1024]{1,0:T(8,128)(2,1)S(1)}, bf16[128,1024]{1,0:T(8,128)(2,1)S(1)}, u32[]{:S(2)}, u32[]{:S(2)}) collective-permute-start(bf16[128,1024]{1,0:T(8,128)(2,1)S(1)} %get-tuple-element.3), channel_id=1, source_target_pairs={{0,128},{128,256},{256,384},{384,0},{1,129},{129,257},{257,385},{3... | collective-permute-start | bytes 786440 | tf_op jit(solution)/shard_map/ppermute | solution.py:24
  105.2 13.5 %collective-permute-start.5 = (bf16[128,1024]{1,0:T(8,128)(2,1)S(1)}, bf16[128,1024]{1,0:T(8,128)(2,1)S(1)}, u32[]{:S(2)}, u32[]{:S(2)}) collective-permute-start(bf16[128,1024]{1,0:T(8,128)(2,1)S(1)} %get-tuple-element.4), channel_id=1, source_target_pairs={{0,256},{128,384},{256,0},{384,128},{1,257},{129,385},{257,1},{385... | collective-permute-start | bytes 786440 | tf_op jit(solution)/shard_map/ppermute | solution.py:24

commit v7 on v6

--- a/solution.py
+++ b/solution.py
@@ -7,7 +7,8 @@
 
 BF16 = jnp.bfloat16
 F32 = jnp.float32
-DP = ("x", "zl", "y")
+Y = ("yq", "yp")
+DP = ("x", "zl") + Y
 MP = ("zh", "core")
 
 
@@ -31,7 +32,7 @@
 
 
 def per_device(query_states, passage_states, proj_weight, positive_index, logit_scale, logit_bias):
-    nx, nzl, ny, nzh = (lax.axis_size(a) for a in ("x", "zl", "y", "zh"))
+    nx, nzl, ny, nzh = (lax.axis_size(a) for a in ("x", "zl", Y, "zh"))
     rows = query_states.shape[0]
     depth, cols = proj_weight.shape
     blocks = nzl * ny
@@ -39,10 +40,11 @@
     scale_value = logit_scale[0]
     bias_value = logit_bias[0]
 
-    w_part = exchange(jnp.broadcast_to(proj_weight[None], (ny, depth, cols)), "y")
-    w_part = w_part.reshape(1, ny * depth, cols)
-    w_all = exchange(jnp.broadcast_to(w_part, (nx * nzl, ny * depth, cols)), ("x", "zl"))
-    w_all = w_all.reshape(nx * blocks * depth, cols)
+    nq, np = lax.axis_size("yq"), lax.axis_size("yp")
+    w_part = exchange(jnp.broadcast_to(proj_weight[None], (nq, depth, cols)), "yq")
+    w_part = jnp.broadcast_to(w_part[None], (nx * nzl * np, nq, depth, cols))
+    w_all = exchange(w_part, ("x", "zl", "yp")).reshape(nx, nzl, np, nq, depth, cols)
+    w_all = w_all.transpose(0, 1, 3, 2, 4, 5).reshape(nx * blocks * depth, cols)
     passages = dot(passage_states, w_all, ((1,), (0,))).astype(BF16)
     queries = dot(query_states, w_all, ((1,), (0,))).astype(BF16)
 
@@ -52,7 +54,7 @@
     p_own = lax.optimization_barrier(own[:, rows:].transpose(1, 0, 2)).reshape(sub, nzh * cols)
     q_own = own[:, :rows].transpose(1, 0, 2).reshape(rows, nzh * cols)
 
-    p_tile = exchange(jnp.broadcast_to(p_own[None], (blocks, sub, nzh * cols)), ("zl", "y"))
+    p_tile = exchange(jnp.broadcast_to(p_own[None], (blocks, sub, nzh * cols)), ("zl",) + Y)
     p_tile = p_tile.reshape(blocks * sub, nzh * cols)
     q_tile = jnp.concatenate([q_own] + [shifted(q_own, "x", k) for k in range(1, nx)], axis=0)
 
@@ -60,7 +62,7 @@
     other = lax.ppermute(part, "core", [(0, 1), (1, 0)])
     scores = part.astype(F32) + other.astype(F32)
 
-    own_block = lax.axis_index("zl") * ny + lax.axis_index("y")
+    own_block = lax.axis_index("zl") * ny + lax.axis_index(Y)
     place = positive_index - lax.axis_index("zh") * sub
     target = jnp.where((place >= 0) & (place < sub), own_block * sub + place, -1)
     target = jnp.pad(target, (0, (nx - 1) * rows), constant_values=-1)[None, :]
@@ -69,7 +71,7 @@
     weight = lax.optimization_barrier((jax.nn.sigmoid(logits) - labels).astype(BF16))
 
     gp = dot(weight, q_tile, ((1,), (0,))).astype(BF16)
-    gp = exchange(gp.reshape(blocks, sub, nzh * cols), ("zl", "y"))
+    gp = exchange(gp.reshape(blocks, sub, nzh * cols), ("zl",) + Y)
     gp = jnp.sum(gp.astype(F32), axis=0)
 
     gq = dot(weight, p_tile, ((0,), (0,)))
@@ -92,7 +94,7 @@
 
 
 def solution(mesh):
-    fine = Mesh(mesh.devices.reshape(4, 2, 8, 4, 2), DP + MP)
+    fine = Mesh(mesh.devices.reshape(4, 2, 4, 2, 4, 2), DP + MP)
     in_specs = (P(DP, None), P(DP, None), P(DP, MP), P(DP), P(), P())
     out_specs = (P(DP, MP), P(DP, MP))
     return jax.shard_map(

time: 141 us -> 140 us (level)
  waiting for transfers between devices: 28 us -> 25.4 us
  starting transfers between devices: 31.6 us -> 33.4 us
    ppermute x6, starting transfers between devices: 17 us -> 19.2 us  [shifted(): lax.ppermute(block, axis, [(i, (i + step) % size) for i in range(size)])]
    all_to_all x2, waiting for transfers between devices: 9.19 us -> 7.29 us  [exchange(): return lax.all_to_all(pieces, axes, 0, 0, tiled=True)]
  transfers between devices with their start and end apart: 9 -> 9, of which waited for: 8 -> 6; matrix products, arithmetic and copies ran while one was open for 1% -> 1% of each run, Pallas kernels for 0% -> 0%
where the time goes in v7:
time: 140 us; the launch traced here: 139 us
  blocking collectives  68.7 us (49%)
  starting transfers between devices  33.4 us (24%)
  waiting for transfers between devices  25.4 us (18%)
  matrix products  4.88 us (3%)
  local copies, waits for them, and re-layouts  3.33 us (2%)
  between operations  2.19 us (2%)
    all_to_all x4, blocking collectives, exchange(): return lax.all_to_all(pieces, axes, 0, 0, tiled=True)  68.7 us
    ppermute x6, starting transfers between devices, shifted(): lax.ppermute(block, axis, [(i, (i + step) % size) for i in range(size)])  19.2 us
    ppermute x6, waiting for transfers between devices, shifted(): lax.ppermute(block, axis, [(i, (i + step) % size) for i in range(size)])  17.6 us
    all_to_all x2, starting transfers between devices, exchange(): return lax.all_to_all(pieces, axes, 0, 0, tiled=True)  12.3 us
    all_to_all x2, waiting for transfers between devices, exchange(): return lax.all_to_all(pieces, axes, 0, 0, tiled=True)  7.29 us
    dot_general x5, matrix products, dot(): lax.dot_general(left, right, (contract, ((), ())), preferred_element_type...  4.88 us
  transfers between devices with their start and end apart: 9, of which 6 were waited for; matrix products, arithmetic and copies ran while one was open for 1% of the time, Pallas kernels for 0%

profile of v7, /device:TPU:16, one launch (start us, length us, event | category | flops | bytes accessed | tf_op | source)
XLA Modules:
  0.0 139.5 jit_solution(15839281923929696848)
XLA Ops:
  0.6 0.8 broadcast_in_dim.13
  1.4 13.9 %all_to_all.30 = bf16[4,32,256]{2,1,0:T(8,128)(2,1)S(1)} all-to-all(bf16[4,32,256]{2,1,0:T(8,128)(2,1)S(1)} %broadcast_in_dim.13), channel_id=1, replica_groups=mesh['x'=4,'zl'=2,'yq'=4,'yp'=2,'zh'=4,'core'=2] {'yq'}, dimensions={0} | all-to-all | bytes 131072 | tf_op jit(solution)/shard_map/all_to_all | solution.py:16
  15.5 19.2 %all_to_all.31 = bf16[16,4,32,256]{3,2,1,0:T(8,128)(2,1)S(1)} all-to-all(bf16[16,4,32,256]{3,2,1,0:T(8,128)(2,1)S(1)} %broadcast_in_dim.14), channel_id=1, replica_groups=mesh['x'=4,'zl'=2,'yq'=4,'yp'=2,'zh'=4,'core'=2] {'x','zl','yp'}, dimensions={0} | all-to-all | bytes 2097152 | tf_op jit(solution)/shard_map/all_to_all | solution.py:16
  36.0 19.8 %all_to_all.32 = bf16[4,160,256]{2,1,0:T(8,128)(2,1)S(1)} all-to-all(bf16[4,160,256]{2,1,0:T(8,128)(2,1)S(1)} %pad_maximum_fusion.1), channel_id=1, replica_groups=mesh['x'=4,'zl'=2,'yq'=4,'yp'=2,'zh'=4,'core'=2] {'zh'}, dimensions={0} | all-to-all | bytes 655360 | tf_op jit(solution)/shard_map/all_to_all | solution.py:16
  55.9 1.1 broadcast_in_dim.18
  57.0 5.7 %all-to-all-start.3 = ((bf16[16,32,1024]{2,1,0:T(8,128)(2,1)}), bf16[16,32,1024]{2,1,0:T(8,128)(2,1)S(1)}, u32[]{:S(2)}, u32[]{:S(2)}) async-start(bf16[16,32,1024]{2,1,0:T(8,128)(2,1)} %broadcast_in_dim.18), calls=%async_computation.3 | async-start | bytes 2097152 | tf_op jit(solution)/shard_map/all_to_all | solution.py:16
  62.9 3.9 %collective-permute-start.2 = (bf16[128,1024]{0,1:T(8,128)(2,1)S(1)}, bf16[128,1024]{0,1:T(8,128)(2,1)S(1)}, u32[]{:S(2)}, u32[]{:S(2)}) collective-permute-start(bf16[128,1024]{0,1:T(8,128)(2,1)S(1)} %bitcast.44), channel_id=1, source_target_pairs={{0,384},{128,0},{256,128},{384,256},{1,385},{129,1},{257,129},{385... | collective-permute-start | bytes 786440 | tf_op jit(solution)/shard_map/ppermute | solution.py:25
  66.8 3.5 %collective-permute-start.1 = (bf16[128,1024]{0,1:T(8,128)(2,1)S(1)}, bf16[128,1024]{0,1:T(8,128)(2,1)S(1)}, u32[]{:S(2)}, u32[]{:S(2)}) collective-permute-start(bf16[128,1024]{0,1:T(8,128)(2,1)S(1)} %bitcast.45), channel_id=1, source_target_pairs={{0,256},{128,384},{256,0},{384,128},{1,257},{129,385},{257,1},{385... | collective-permute-start | bytes 786440 | tf_op jit(solution)/shard_map/ppermute | solution.py:25
  70.3 1.9 %collective-permute-start = (bf16[128,1024]{0,1:T(8,128)(2,1)S(1)}, bf16[128,1024]{0,1:T(8,128)(2,1)S(1)}, u32[]{:S(2)}, u32[]{:S(2)}) collective-permute-start(bf16[128,1024]{0,1:T(8,128)(2,1)S(1)} %bitcast.46), channel_id=1, source_target_pairs={{0,128},{128,256},{256,384},{384,0},{1,129},{129,257},{257,385},{3... | collective-permute-start | bytes 786440 | tf_op jit(solution)/shard_map/ppermute | solution.py:25
  72.3 4.3 %collective-permute-done.1 = bf16[128,1024]{0,1:T(8,128)(2,1)S(1)} collective-permute-done((bf16[128,1024]{0,1:T(8,128)(2,1)S(1)}, bf16[128,1024]{0,1:T(8,128)(2,1)S(1)}, u32[]{:S(2)}, u32[]{:S(2)}) %collective-permute-start.1) | collective-permute-done | bytes 262176 | tf_op jit(solution)/shard_map/ppermute | solution.py:25
  76.6 3.2 %collective-permute-done = bf16[128,1024]{0,1:T(8,128)(2,1)S(1)} collective-permute-done((bf16[128,1024]{0,1:T(8,128)(2,1)S(1)}, bf16[128,1024]{0,1:T(8,128)(2,1)S(1)}, u32[]{:S(2)}, u32[]{:S(2)}) %collective-permute-start) | collective-permute-done | bytes 262176 | tf_op jit(solution)/shard_map/ppermute | solution.py:25
  79.8 3.8 %all-to-all-done.3 = bf16[16,32,1024]{2,1,0:T(8,128)(2,1)S(1)} async-done(((bf16[16,32,1024]{2,1,0:T(8,128)(2,1)}), bf16[16,32,1024]{2,1,0:T(8,128)(2,1)S(1)}, u32[]{:S(2)}, u32[]{:S(2)}) %all-to-all-start.3) | async-done | bytes 1048608 | tf_op jit(solution)/shard_map/all_to_all | solution.py:16
  83.6 0.7 convolution_convert_fusion.1
  84.4 1.9 %collective-permute-start.3 = (bf16[512,512]{1,0:T(8,128)(2,1)S(1)}, bf16[512,512]{1,0:T(8,128)(2,1)S(1)}, u32[]{:S(2)}, u32[]{:S(2)}) collective-permute-start(bf16[512,512]{1,0:T(8,128)(2,1)S(1)} %convolution_convert_fusion.1), channel_id=1, source_target_pairs={{0,1},{1,0},{2,3},{3,2},{4,5},{5,4},{6,7},{7,6},{8,9},{9,8},{10,11... | collective-permute-start | bytes 1572872 | tf_op jit(solution)/shard_map/ppermute | solution.py:62
  88.6 2.8 %convolution_convert_fusion = bf16[512,1024]{1,0:T(8,128)(2,1)} fusion(bf16[512,512]{1,0:T(8,128)(2,1)S(1)} %subtract_convert_fusion, bf16[128,1024]{0,1:T(8,128)(2,1)} %copy-done.3, bf16[128,1024]{0,1:T(8,128)(2,1)} %copy-done.4, bf16[128,1024]{0,1:T(8,128)(2,1)} %copy-done.5, bf16[128,1024]{0,1:T(8,128)(2,1)S(1)} %bitcast.48), kind=kOutput, calls=%fused_computation | convolution fusion | flops 541589504 | bytes 2621440 | tf_op jit(solution)/shard_map/dot_general | solution.py:20
  91.5 6.6 %all-to-all-start.4 = ((bf16[16,32,1024]{2,1,0:T(8,128)(2,1)}), bf16[16,32,1024]{2,1,0:T(8,128)(2,1)S(1)}, u32[]{:S(2)}, u32[]{:S(2)}) async-start(bf16[16,32,1024]{2,1,0:T(8,128)(2,1)} %bitcast.38), calls=%async_computation.4 | async-start | bytes 2097152 | tf_op jit(solution)/shard_map/all_to_all | solution.py:16
  98.1 0.7 fusion.4
  98.9 3.7 %collective-permute-start.4 = (bf16[128,1024]{1,0:T(8,128)(2,1)S(1)}, bf16[128,1024]{1,0:T(8,128)(2,1)S(1)}, u32[]{:S(2)}, u32[]{:S(2)}) collective-permute-start(bf16[128,1024]{1,0:T(8,128)(2,1)S(1)} %get-tuple-element.2), channel_id=1, source_target_pairs={{0,384},{128,0},{256,128},{384,256},{1,385},{129,1},{257,129},{385... | collective-permute-start | bytes 786440 | tf_op jit(solution)/shard_map/ppermute | solution.py:25
  102.6 2.2 %collective-permute-start.6 = (bf16[128,1024]{1,0:T(8,128)(2,1)S(1)}, bf16[128,1024]{1,0:T(8,128)(2,1)S(1)}, u32[]{:S(2)}, u32[]{:S(2)}) collective-permute-start(bf16[128,1024]{1,0:T(8,128)(2,1)S(1)} %get-tuple-element.3), channel_id=1, source_target_pairs={{0,128},{128,256},{256,384},{384,0},{1,129},{129,257},{257,385},{3... | collective-permute-start | bytes 786440 | tf_op jit(solution)/shard_map/ppermute | solution.py:25
  104.7 4.0 %collective-permute-start.5 = (bf16[128,1024]{1,0:T(8,128)(2,1)S(1)}, bf16[128,1024]{1,0:T(8,128)(2,1)S(1)}, u32[]{:S(2)}, u32[]{:S(2)}) collective-permute-start(bf16[128,1024]{1,0:T(8,128)(2,1)S(1)} %get-tuple-element.4), channel_id=1, source_target_pairs={{0,256},{128,384},{256,0},{384,128},{1,257},{129,385},{257,1},{385... | collective-permute-start | bytes 786440 | tf_op jit(solution)/shard_map/ppermute | solution.py:25
  108.7 10.1 %collective-permute-done.6 = bf16[128,1024]{1,0:T(8,128)(2,1)S(1)} collective-permute-done((bf16[128,1024]{1,0:T(8,128)(2,1)S(1)}, bf16[128,1024]{1,0:T(8,128)(2,1)S(1)}, u32[]{:S(2)}, u32[]{:S(2)}) %collective-permute-start.6) | collective-permute-done | bytes 262176 | tf_op jit(solution)/shard_map/ppermute | solution.py:25
  119.3 3.5 %all-to-all-done.4 = bf16[16,32,1024]{2,1,0:T(8,128)(2,1)S(1)} async-done(((bf16[16,32,1024]{2,1,0:T(8,128)(2,1)}), bf16[16,32,1024]{2,1,0:T(8,128)(2,1)S(1)}, u32[]{:S(2)}, u32[]{:S(2)}) %all-to-all-start.4) | async-done | bytes 1048608 | tf_op jit(solution)/shard_map/all_to_all | solution.py:16
  123.0 15.7 %all_to_all.33.both = bf16[4,160,256]{2,1,0:T(8,128)(2,1)S(1)} all-to-all(bf16[4,160,256]{2,1,0:T(8,128)(2,1)S(1)} %maximum_bitcast_fusion), channel_id=1, replica_groups=mesh['x'=4,'zl'=2,'yq'=4,'yp'=2,'zh'=4,'core'=2] {'zh'}, dimensions={0} | all-to-all | bytes 655360 | tf_op jit(solution)/shard_map/all_to_all | solution.py:16
  138.7 0.7 shard_map.77
  (36 shorter events, 3.5 us)
Async XLA Ops:
  0.6 34.1 %copy-start = (bf16[128,2048]{1,0:T(8,128)(2,1)S(1)}, bf16[128,2048]{1,0:T(8,128)(2,1)}, u32[]{:S(2)}) copy-start(bf16[128,2048]{1,0:T(8,128)(2,1)} %param.7) | copy-start | bytes 1572868
  34.6 1.0 copy-start.1
  57.0 26.6 %all-to-all-start.3 = ((bf16[16,32,1024]{2,1,0:T(8,128)(2,1)}), bf16[16,32,1024]{2,1,0:T(8,128)(2,1)S(1)}, u32[]{:S(2)}, u32[]{:S(2)}) async-start(bf16[16,32,1024]{2,1,0:T(8,128)(2,1)} %broadcast_in_dim.18), calls=%async_computation.3 | async-start | bytes 2097152 | tf_op jit(solution)/shard_map/all_to_all | solution.py:16
  62.9 9.4 %collective-permute-start.2 = (bf16[128,1024]{0,1:T(8,128)(2,1)S(1)}, bf16[128,1024]{0,1:T(8,128)(2,1)S(1)}, u32[]{:S(2)}, u32[]{:S(2)}) collective-permute-start(bf16[128,1024]{0,1:T(8,128)(2,1)S(1)} %bitcast.44), channel_id=1, source_target_pairs={{0,384},{128,0},{256,128},{384,256},{1,385},{129,1},{257,129},{385... | collective-permute-start | bytes 786440 | tf_op jit(solution)/shard_map/ppermute | solution.py:25
  66.8 9.8 %collective-permute-start.1 = (bf16[128,1024]{0,1:T(8,128)(2,1)S(1)}, bf16[128,1024]{0,1:T(8,128)(2,1)S(1)}, u32[]{:S(2)}, u32[]{:S(2)}) collective-permute-start(bf16[128,1024]{0,1:T(8,128)(2,1)S(1)} %bitcast.45), channel_id=1, source_target_pairs={{0,256},{128,384},{256,0},{384,128},{1,257},{129,385},{257,1},{385... | collective-permute-start | bytes 786440 | tf_op jit(solution)/shard_map/ppermute | solution.py:25
  70.3 9.5 %collective-permute-start = (bf16[128,1024]{0,1:T(8,128)(2,1)S(1)}, bf16[128,1024]{0,1:T(8,128)(2,1)S(1)}, u32[]{:S(2)}, u32[]{:S(2)}) collective-permute-start(bf16[128,1024]{0,1:T(8,128)(2,1)S(1)} %bitcast.46), channel_id=1, source_target_pairs={{0,128},{128,256},{256,384},{384,0},{1,129},{129,257},{257,385},{3... | collective-permute-start | bytes 786440 | tf_op jit(solution)/shard_map/ppermute | solution.py:25
  72.3 11.4 %copy-start.3 = (bf16[128,1024]{0,1:T(8,128)(2,1)}, bf16[128,1024]{0,1:T(8,128)(2,1)S(1)}, u32[]{:S(2)}) copy-start(bf16[128,1024]{0,1:T(8,128)(2,1)S(1)} %collective-permute-done.2) | copy-start | bytes 786436
  76.6 7.0 %copy-start.4 = (bf16[128,1024]{0,1:T(8,128)(2,1)}, bf16[128,1024]{0,1:T(8,128)(2,1)S(1)}, u32[]{:S(2)}) copy-start(bf16[128,1024]{0,1:T(8,128)(2,1)S(1)} %collective-permute-done.1) | copy-start | bytes 786436
  79.8 4.6 %copy-start.5 = (bf16[128,1024]{0,1:T(8,128)(2,1)}, bf16[128,1024]{0,1:T(8,128)(2,1)S(1)}, u32[]{:S(2)}) copy-start(bf16[128,1024]{0,1:T(8,128)(2,1)S(1)} %collective-permute-done) | copy-start | bytes 786436
  83.6 4.0 %copy-start.2 = (s32[128]{0:T(128)S(1)}, s32[128]{0:T(128)}, u32[]{:S(2)}) copy-start(s32[128]{0:T(128)} %param.9) | copy-start | bytes 1540
  84.4 3.8 %collective-permute-start.3 = (bf16[512,512]{1,0:T(8,128)(2,1)S(1)}, bf16[512,512]{1,0:T(8,128)(2,1)S(1)}, u32[]{:S(2)}, u32[]{:S(2)}) collective-permute-start(bf16[512,512]{1,0:T(8,128)(2,1)S(1)} %convolution_convert_fusion.1), channel_id=1, source_target_pairs={{0,1},{1,0},{2,3},{3,2},{4,5},{5,4},{6,7},{7,6},{8,9},{9,8},{10,11... | collective-permute-start | bytes 1572872 | tf_op jit(solution)/shard_map/ppermute | solution.py:62
  91.5 31.3 %all-to-all-start.4 = ((bf16[16,32,1024]{2,1,0:T(8,128)(2,1)}), bf16[16,32,1024]{2,1,0:T(8,128)(2,1)S(1)}, u32[]{:S(2)}, u32[]{:S(2)}) async-start(bf16[16,32,1024]{2,1,0:T(8,128)(2,1)} %bitcast.38), calls=%async_computation.4 | async-start | bytes 2097152 | tf_op jit(solution)/shard_map/all_to_all | solution.py:16
  98.9 9.8 %collective-permute-start.4 = (bf16[128,1024]{1,0:T(8,128)(2,1)S(1)}, bf16[128,1024]{1,0:T(8,128)(2,1)S(1)}, u32[]{:S(2)}, u32[]{:S(2)}) collective-permute-start(bf16[128,1024]{1,0:T(8,128)(2,1)S(1)} %get-tuple-element.2), channel_id=1, source_target_pairs={{0,384},{128,0},{256,128},{384,256},{1,385},{129,1},{257,129},{385... | collective-permute-start | bytes 786440 | tf_op jit(solution)/shard_map/ppermute | solution.py:25
  102.6 16.2 %collective-permute-start.6 = (bf16[128,1024]{1,0:T(8,128)(2,1)S(1)}, bf16[128,1024]{1,0:T(8,128)(2,1)S(1)}, u32[]{:S(2)}, u32[]{:S(2)}) collective-permute-start(bf16[128,1024]{1,0:T(8,128)(2,1)S(1)} %get-tuple-element.3), channel_id=1, source_target_pairs={{0,128},{128,256},{256,384},{384,0},{1,129},{129,257},{257,385},{3... | collective-permute-start | bytes 786440 | tf_op jit(solution)/shard_map/ppermute | solution.py:25
  104.7 14.1 %collective-permute-start.5 = (bf16[128,1024]{1,0:T(8,128)(2,1)S(1)}, bf16[128,1024]{1,0:T(8,128)(2,1)S(1)}, u32[]{:S(2)}, u32[]{:S(2)}) collective-permute-start(bf16[128,1024]{1,0:T(8,128)(2,1)S(1)} %get-tuple-element.4), channel_id=1, source_target_pairs={{0,256},{128,384},{256,0},{384,128},{1,257},{129,385},{257,1},{385... | collective-permute-start | bytes 786440 | tf_op jit(solution)/shard_map/ppermute | solution.py:25
